TPU v7x, 256 devices: a whole 4x4x8 slice. The times are simulated.
256 devices in a mesh: depth: 8 (over z_hi, core), eta: 32 (over x, z_lo, y).
Axes of the slice: x: 4, y: 4, z: 8 (z_hi: 4, z_lo: 2; z = z_hi * 2 + z_lo), core: 2. Of those that a mesh axis runs over, the one named last changes fastest.
Arguments:
- field_in: bfloat16 [16, 128, 32, 2048], P('depth', 'eta'), may hold values from -6 to 6
- grad_out: bfloat16 [16, 128, 32, 2048], P('depth', 'eta'), may hold values from -6 to 6
- spectral_weight: bfloat16 [2, 64, 64, 1024], P(None, 'eta'), may hold values from -0.75 to 0.75
- mlp_in: bfloat16 [32, 64], replicated, may hold values from -1 to 1
- mlp_bias: float32 [64], replicated, may hold values from -3 to 3
- mlp_out: bfloat16 [64, 32], replicated, may hold values from -0.75 to 0.75
Outputs:
- grad_in: float32 [16, 128, 32, 2048], P('depth', 'eta')
- grad_spectral: float32 [2, 64, 64, 1024], P(None, 'eta', 'depth')
- grad_mlp_in: float32 [32, 64], replicated
- grad_mlp_out: float32 [64, 32], replicated
- grad_mlp_bias: float32 [64], replicated
All inputs are finite; a program needn't handle non-finite values.
Results may differ from a plain program's by a relative error of at most 0.0087.
Values may be sent and summed in bfloat16 or wider, within the bound.
A program may use at most 128 MiB of HBM per device.

v0:
```python
import math

import jax
import jax.numpy as jnp
from jax import lax
from jax.sharding import PartitionSpec as P


def phi_tables(n_phi, n_modes):
    cells = jnp.arange(n_phi, dtype=jnp.int32)
    index = jnp.arange(n_modes, dtype=jnp.int32)
    freq = jnp.where(index < n_modes // 2, index, n_phi - n_modes + index)
    theta = 2.0 * math.pi / n_phi * (cells[:, None] * freq[None, :] % n_phi).astype(jnp.float32)
    pairs = jnp.stack([jnp.cos(theta), -jnp.sin(theta)], axis=-1).reshape(n_phi, 2 * n_modes)
    forward = (pairs / math.sqrt(n_phi)).astype(jnp.bfloat16)
    inverse = (pairs.T / math.sqrt(n_modes)).astype(jnp.bfloat16)
    return (forward, inverse)


def eta_tables(n_eta, n_modes, start, count):
    cells = start + jnp.arange(count, dtype=jnp.int32)
    index = jnp.arange(n_modes, dtype=jnp.int32)
    phase = 2.0 * math.pi / n_eta * (cells[:, None] * index[None, :] % n_eta).astype(jnp.float32)
    cosine = jnp.cos(phase)
    sine = jnp.sin(phase)
    return (
        (cosine / math.sqrt(n_eta)).astype(jnp.bfloat16),
        (sine / math.sqrt(n_eta)).astype(jnp.bfloat16),
        cosine.T / math.sqrt(n_modes),
        sine.T / math.sqrt(n_modes),
    )


def gelu_slope(value):
    normal_cdf = 0.5 * (1.0 + lax.erf(value / math.sqrt(2.0)))
    return normal_cdf + value * jnp.exp(-0.5 * value * value) / math.sqrt(2.0 * math.pi)


def eta_forward(spectra, eta_cos, eta_sin):
    layers, cells, chans, twice = spectra.shape
    parts = spectra.reshape(layers, cells, chans, twice // 2, 2)
    real_part = parts[..., 0]
    imag_part = parts[..., 1]
    f32 = jnp.float32
    zr = jnp.einsum("decj,em->jdmc", real_part, eta_cos, preferred_element_type=f32) + jnp.einsum(
        "decj,em->jdmc", imag_part, eta_sin, preferred_element_type=f32
    )
    zi = jnp.einsum("decj,em->jdmc", imag_part, eta_cos, preferred_element_type=f32) - jnp.einsum(
        "decj,em->jdmc", real_part, eta_sin, preferred_element_type=f32
    )
    return jnp.stack([zr, zi], axis=2)


def eta_inverse(modes, inv_cos, inv_sin):
    hp = lax.Precision.HIGHEST
    vr = modes[:, :, 0]
    vi = modes[:, :, 1]
    wr = jnp.einsum("jdmc,me->decj", vr, inv_cos, precision=hp) - jnp.einsum(
        "jdmc,me->decj", vi, inv_sin, precision=hp
    )
    wi = jnp.einsum("jdmc,me->decj", vr, inv_sin, precision=hp) + jnp.einsum(
        "jdmc,me->decj", vi, inv_cos, precision=hp
    )
    layers, cells, chans, count = wr.shape
    return (
        jnp.stack([wr, wi], axis=-1).reshape(layers, cells, chans, 2 * count).astype(jnp.bfloat16)
    )


def local(field_in, grad_out, spectral_weight, mlp_in, mlp_bias, mlp_out):
    hp = lax.Precision.HIGHEST
    f32 = jnp.float32
    layers, eta_local, chans, n_phi = field_in.shape
    eta_count = lax.axis_size("eta")
    n_eta = eta_local * eta_count
    owned = spectral_weight.shape[1]
    n_phi_modes = owned * eta_count
    n_eta_modes = spectral_weight.shape[2]
    phi_fwd, phi_inv = phi_tables(n_phi, n_phi_modes)
    weights = spectral_weight.reshape(2, owned, n_eta_modes, chans, chans).astype(f32)
    rr = weights[0]
    ri = weights[1]
    first = lax.axis_index("eta") * eta_local
    eta_cos, eta_sin, inv_cos, inv_sin = eta_tables(n_eta, n_eta_modes, first, eta_local)

    def to_modes(spectra):
        return lax.psum_scatter(
            eta_forward(spectra, eta_cos, eta_sin), "eta", scatter_dimension=0, tiled=True
        )

    def from_modes(modes):
        fields = eta_inverse(lax.all_gather(modes, "eta", axis=0, tiled=True), inv_cos, inv_sin)
        return jnp.dot(fields, phi_inv, preferred_element_type=f32)

    xp = jnp.dot(field_in, phi_fwd, preferred_element_type=f32).astype(jnp.bfloat16)
    zx = to_modes(xp)
    zr = zx[:, :, 0]
    zi = zx[:, :, 1]
    vr = jnp.einsum("kdmc,kmco->kdmo", zr, rr, precision=hp) - jnp.einsum(
        "kdmc,kmco->kdmo", zi, ri, precision=hp
    )
    vi = jnp.einsum("kdmc,kmco->kdmo", zr, ri, precision=hp) + jnp.einsum(
        "kdmc,kmco->kdmo", zi, rr, precision=hp
    )
    spectral = from_modes(jnp.stack([vr, vi], axis=2))
    hidden_pre = (
        jnp.einsum("decp,ch->dehp", field_in, mlp_in, preferred_element_type=f32)
        + mlp_bias[None, None, :, None]
    )
    hidden = jax.nn.gelu(hidden_pre, approximate=False).astype(jnp.bfloat16)
    pre = spectral + jnp.einsum("dehp,hc->decp", hidden, mlp_out, preferred_element_type=f32)
    gpre = (grad_out.astype(f32) * gelu_slope(pre)).astype(jnp.bfloat16)
    gp = jnp.dot(gpre, phi_fwd, preferred_element_type=f32).astype(jnp.bfloat16)
    zg = to_modes(gp)
    gr = zg[:, :, 0]
    gi = zg[:, :, 1]
    local_r = jnp.einsum("kdmc,kdmo->kmco", zr, gr, precision=hp) + jnp.einsum(
        "kdmc,kdmo->kmco", zi, gi, precision=hp
    )
    local_i = jnp.einsum("kdmc,kdmo->kmco", zr, gi, precision=hp) - jnp.einsum(
        "kdmc,kdmo->kmco", zi, gr, precision=hp
    )
    local_grad = jnp.stack([local_r, local_i], axis=0).reshape(2, owned, n_eta_modes, chans * chans)
    factor = math.sqrt(n_phi * n_eta / (n_phi_modes * n_eta_modes))
    grad_spectral = lax.psum_scatter(local_grad, "depth", scatter_dimension=2, tiled=True) * factor
    br = jnp.einsum("kdmo,kmco->kdmc", gr, rr, precision=hp) + jnp.einsum(
        "kdmo,kmco->kdmc", gi, ri, precision=hp
    )
    bi = jnp.einsum("kdmo,kmco->kdmc", gi, rr, precision=hp) - jnp.einsum(
        "kdmo,kmco->kdmc", gr, ri, precision=hp
    )
    back_spec = from_modes(jnp.stack([br, bi], axis=2))
    hidden_grad = jnp.einsum(
        "decp,hc->dehp", gpre, mlp_out, preferred_element_type=f32
    ) * gelu_slope(hidden_pre)
    hidden_gb = hidden_grad.astype(jnp.bfloat16)
    grad_in = (
        grad_out.astype(f32)
        + back_spec
        + jnp.einsum("dehp,ch->decp", hidden_gb, mlp_in, preferred_element_type=f32)
    )
    part_in = jnp.einsum("decp,dehp->ch", field_in, hidden_gb, preferred_element_type=f32)
    part_out = jnp.einsum("dehp,decp->hc", hidden, gpre, preferred_element_type=f32)
    part_bias = jnp.sum(hidden_grad, axis=(0, 1, 3))
    total_in, total_out, total_bias = lax.psum((part_in, part_out, part_bias), ("depth", "eta"))
    norm = 1.0 / math.sqrt(layers * lax.axis_size("depth") * n_eta * n_phi)
    return (grad_in, grad_spectral, total_in * norm, total_out * norm, total_bias * norm)


def solution(mesh):
    return jax.shard_map(
        local,
        mesh=mesh,
        in_specs=(
            P("depth", "eta", None, None),
            P("depth", "eta", None, None),
            P(None, "eta", None, None),
            P(),
            P(),
            P(),
        ),
        out_specs=(P("depth", "eta", None, None), P(None, "eta", "depth", None), P(), P(), P()),
        check_vma=False,
    )
```

profile of v0, /device:TPU:64, one launch (start us, length us, event | category | flops | bytes accessed | tf_op | source)
XLA Modules:
  0.0 928.1 jit_solution(8209441695494831435)
XLA Ops:
  17.4 6.3 copy.137
  30.3 166.7 %reduce-scatter.3.cloned.1.call-done = f32[2,2,2,64,32]{3,4,2,1,0:T(8,128)} async-done(((f32[64,2,2,64,32]{3,4,2,1,0:T(8,128)}), f32[2,2,2,64,32]{3,4,2,1,0:T(8,128)}) %reduce-scatter.3.cloned.1.call-update) | async-done | bytes 65552 | tf_op jit(solution)/shard_map/reduce_scatter | solution.py:87
  205.7 10.8 %fusion.2 = (bf16[2,4,64,2048]{3,2,1,0:T(8,128)(2,1)}, f32[64,2,4,2048]{3,0,2,1:T(8,128)}) fusion(f32[64]{0:T(128)S(1)} %copy-done.16, bf16[2,4,32,2048]{3,2,1,0:T(8,128)(2,1)S(1)} %copy-done, bf16[32,64]{1,0:T(8,128)(2,1)S(1)} %copy-done.14), kind=kOutput, calls=%fused_computation.4 | convolution fusion | flops 136314880 | bytes 7344384 | tf_op jit(solution)/shard_map/decp,ch->dehp/dot_general | solution.py:107
  216.5 151.7 %all-gather.3.cloned.1.call-done = f32[64,2,2,64,32]{4,1,3,0,2:T(2,128)} async-done(((f32[2,2,2,64,32]{4,1,3,0,2:T(2,128)}), f32[64,2,2,64,32]{4,1,3,0,2:T(2,128)}) %all-gather.3.cloned.1.call-update) | async-done | bytes 2097168 | tf_op jit(solution)/shard_map/all_gather | solution.py:92
  368.2 7.8 slice_bitcast_fusion.2
  376.0 5.4 copy.146
  381.4 5.0 fusion.111
  386.4 5.0 fusion.104
  391.4 5.9 copy.147
  397.4 5.0 fusion.41
  402.4 5.0 fusion.40
  423.6 6.3 copy.158
  430.2 170.9 %reduce-scatter.5.cloned.1.call-done = f32[2,2,2,64,32]{3,4,2,1,0:T(8,128)} async-done(((f32[64,2,2,64,32]{3,4,2,1,0:T(8,128)}), f32[2,2,2,64,32]{3,4,2,1,0:T(8,128)}) %reduce-scatter.5.cloned.1.call-update) | async-done | bytes 65552 | tf_op jit(solution)/shard_map/reduce_scatter | solution.py:87
  602.1 4.8 fusion.63
  610.5 6.1 convolution_add_fusion.1
  653.6 74.3 %all-reduce.1 = (f32[32,64]{1,0:T(8,128)S(1)}, f32[64,32]{0,1:T(8,128)S(1)}, f32[64]{0:T(128)S(1)}) all-reduce(f32[32,64]{1,0:T(8,128)S(1)} %convolution_bitcast_fusion.3, f32[64,32]{0,1:T(8,128)S(1)} %convolution_bitcast_fusion.2, f32[64]{0:T(128)S(1)} %get-tuple-element.43), channel_id=1, replica_groups=mesh['depth'=8,'eta'=32] {'depth','eta'}, use_global_device_ids=true, to_apply=%region_3.4 | all-reduce | flops 4160 | bytes 33280 | tf_op jit(solution)/shard_map/psum | solution.py:145
  731.3 146.4 %all-gather.5.cloned.1.call-done = f32[64,2,2,64,32]{4,1,3,0,2:T(2,128)} async-done(((f32[2,2,2,64,32]{4,1,3,0,2:T(2,128)}), f32[64,2,2,64,32]{4,1,3,0,2:T(2,128)}) %all-gather.5.cloned.1.call-update) | async-done | bytes 2097168 | tf_op jit(solution)/shard_map/all_gather | solution.py:92
  877.8 7.8 slice_bitcast_fusion
  885.6 5.4 copy.165
  891.0 5.0 fusion.108
  896.0 5.0 fusion.101
  901.0 5.8 copy.166
  906.8 5.0 fusion.39
  911.8 5.0 fusion.38
  (117 shorter events, 89.9 us)
Async XLA Ops:
  7.2 4.0 copy-start
  7.2 189.8 %reduce-scatter.3.cloned.1.call-start = ((), (), s32[]{:S(2)}) async-start(), calls=%async_computation.2 | async-start | bytes 4325376 | tf_op jit(solution)/shard_map/reduce_scatter | solution.py:87
  11.1 3.2 copy-start.5
  23.8 1.0 copy-start.13
  23.8 344.4 %all-gather.3.cloned.1.call-start = ((), (), s32[]{:S(2)}) async-start(), calls=%async_computation.3 | async-start | bytes 8650752 | tf_op jit(solution)/shard_map/all_gather | solution.py:92
  26.6 175.2 %copy-start.1 = (bf16[2,64,32,32]{3,2,1,0:T(8,128)(2,1)}, bf16[2,64,32,32]{3,2,1,0:T(8,128)(2,1)S(1)}, u32[]{:S(2)}) copy-start(bf16[2,64,32,32]{3,2,1,0:T(8,128)(2,1)S(1)} %copy.140) | copy-start | bytes 786436
  30.3 175.4 %copy-start.7 = (bf16[2,64,32,32]{3,2,1,0:T(8,128)(2,1)}, bf16[2,64,32,32]{3,2,1,0:T(8,128)(2,1)S(1)}, u32[]{:S(2)}) copy-start(bf16[2,64,32,32]{3,2,1,0:T(8,128)(2,1)S(1)} %copy.143) | copy-start | bytes 786436
  198.1 7.6 copy-start.10
  198.1 7.6 copy-start.14
  198.1 7.6 copy-start.16
  202.8 398.4 %reduce-scatter.5.cloned.1.call-start = ((), (), s32[]{:S(2)}) async-start(), calls=%async_computation.4 | async-start | bytes 4325376 | tf_op jit(solution)/shard_map/reduce_scatter | solution.py:87
  402.4 6.9 copy-start.15
  409.2 4.3 copy-start.6
  412.6 1.0 copy-start.9
  417.6 2.9 copy-start.12
  430.0 299.6 %all-reduce.4.cloned.1.call-start = ((), (), s32[]{:S(2)}) async-start(), calls=%async_computation.6 | async-start | bytes 2097152
  610.5 9.7 %copy-start.11 = (f32[2,2,1,64,32]{4,1,3,0,2:T(2,128)S(1)}, f32[2,2,1,64,32]{4,1,3,0,2:T(2,128)}, u32[]{:S(2)}) copy-start(f32[2,2,1,64,32]{4,1,3,0,2:T(2,128)} %copy-done.10) | copy-start | bytes 98308
  628.6 6.3 copy-start.2
  628.6 8.0 copy-start.8
  634.6 243.2 %all-gather.5.cloned.1.call-start = ((), (), s32[]{:S(2)}) async-start(), calls=%async_computation.5 | async-start | bytes 8650752 | tf_op jit(solution)/shard_map/all_gather | solution.py:92
  651.5 1.3 copy-start.3
  916.9 2.3 copy-start.4
Sparse Core Ops, SparseCore 0:
  23.9 173.0 reduce-scatter.2
  202.9 165.2 all-gather.2
  430.1 170.9 reduce-scatter.4
  634.7 69.0 all-reduce.3
  705.5 172.2 all-gather.4
where the time goes:
time: 935 us; the launch traced here: 928 us
  waiting for transfers between devices  636 us (68%)
  matrix products  105 us (11%)
  local copies, waits for them, and re-layouts  80.2 us (9%)
  blocking collectives  74.3 us (8%)
  other arithmetic  15.9 us (2%)
  between operations  15.5 us (2%)
    reduce_scatter x2, waiting for transfers between devices, to_modes(): lax.psum_scatter(eta_forward(spectra, eta_cos, eta_sin), 'eta', scatter_d...  338 us
    all_gather x2, waiting for transfers between devices, from_modes(): lax.all_gather(modes, 'eta', axis=0, tiled=True)  298 us
    psum x1, blocking collectives, local(): lax.psum((part_in, part_out, part_bias), ('depth', 'eta'))  74.3 us
    squeeze x4, local copies, waits for them, and re-layouts, eta_inverse(): vi = modes[:, :, 1]  27.2 us
  transfers between devices with their start and end apart: 5, of which 4 were waited for; matrix products, arithmetic and copies ran while one was open for 4% of the time, Pallas kernels for 0%

commit v1 on v0

v1 whole, which is shorter than its diff:
```python
import functools
import math

import jax
import jax.numpy as jnp
import ml_dtypes
import numpy as np
from jax import lax
from jax.experimental import pallas as pl
from jax.experimental.pallas import tpu as pltpu
from jax.sharding import PartitionSpec as P

F32 = jnp.float32
BF16 = jnp.bfloat16
MESH = pl.DeviceIdType.MESH


def bf(table):
    return table.astype(np.float32).astype(ml_dtypes.bfloat16)


def phi_table(n_phi, n_modes):
    owners = n_modes // 2
    mode = 2 * np.arange(owners)[None, :] + np.arange(2)[:, None]
    freq = np.where(mode < n_modes // 2, mode, n_phi - n_modes + mode)
    theta = 2.0 * np.pi / n_phi * ((freq[:, :, None] * np.arange(n_phi)) % n_phi)
    pairs = np.stack([np.cos(theta), -np.sin(theta)], axis=1).reshape(4 * owners, n_phi)
    return bf(pairs / math.sqrt(n_phi)), bf(pairs / math.sqrt(n_modes))


def eta_tables(n_eta, n_modes, owners):
    j, hi, lo = np.meshgrid(np.arange(owners), np.arange(2), np.arange(2), indexing="ij")
    cell = 4 * j + 2 * hi + lo
    phase = 2.0 * np.pi / n_eta * ((cell[..., None] * np.arange(n_modes)) % n_eta)
    cosine, sine = np.cos(phase), np.sin(phase)
    fwd = np.zeros((2, owners, 2, 2, 2, 2, 2, n_modes))
    inv = np.zeros((owners, 2, 2, 2, 2, 2, 2, n_modes))
    for low in range(2):
        c, s = cosine[:, :, low], sine[:, :, low]
        for kk in range(2):
            fwd[low, :, kk, 0, :, 0, kk] = c
            fwd[low, :, kk, 1, :, 0, kk] = s
            fwd[low, :, kk, 0, :, 1, kk] = -s
            fwd[low, :, kk, 1, :, 1, kk] = c
            inv[:, kk, 0, :, low, 0, kk] = c
            inv[:, kk, 0, :, low, 1, kk] = -s
            inv[:, kk, 1, :, low, 0, kk] = s
            inv[:, kk, 1, :, low, 1, kk] = c
    fwd = fwd.reshape(2 * 8 * owners, 4 * n_modes) / math.sqrt(n_eta)
    inv = inv.reshape(8 * owners, 8 * n_modes) / math.sqrt(n_modes)
    return bf(fwd), bf(inv)


def nn(a, b):
    return lax.dot_general(a, b, (((1,), (0,)), ((), ())), preferred_element_type=F32)


def nt(a, b):
    return lax.dot_general(a, b, (((1,), (1,)), ((), ())), preferred_element_type=F32)


def cdf_and_density(v):
    cdf = 0.5 + 0.5 * lax.erf(v * (1.0 / math.sqrt(2.0)))
    density = jnp.exp(-0.5 * v * v) * (1.0 / math.sqrt(2.0 * math.pi))
    return cdf, density


def eta_order(x):
    blocks = [x[b * 32 : (b + 1) * 32] for b in range(8)]
    return jnp.concatenate([blocks[d * 4 + hi * 2 + lo] for hi in range(2) for lo in range(2) for d in range(2)], axis=0)


def cell_order(x):
    blocks = [x[b * 32 : (b + 1) * 32] for b in range(8)]
    return jnp.concatenate([blocks[hi * 4 + lo * 2 + d] for d in range(2) for hi in range(2) for lo in range(2)], axis=0)


def kernel(
    n_dep,
    n_eta,
    chunk,
    factor,
    norm,
    field_hbm,
    cotan_hbm,
    weight_hbm,
    mlp_in,
    mlp_bias,
    mlp_out,
    fwd_hbm,
    inv_hbm,
    efwd_hbm,
    einv_hbm,
    gin_hbm,
    gspec,
    out_in,
    out_out,
    out_bias,
    field,
    cotan,
    weight,
    tfwd,
    tinv,
    efwd,
    einv,
    hid,
    slope,
    part,
    gpre,
    w_all,
    m_up,
    m_down,
    m_outt,
    m_out,
    bias_col,
    rt,
    rt2,
    zbuf,
    vsend,
    sends,
    recvs,
    dsend,
    drecv,
    xexp,
    gexp,
    asend,
    arecv,
    bsend,
    brecv,
    csend,
    crecv,
    load_sem,
    out_sem,
    send_sem,
    recv_sem,
):
    dep = lax.axis_index("depth")
    eta = lax.axis_index("eta")
    n_phi = field.shape[1]
    n_chunks = n_phi // chunk

    barrier = pltpu.get_barrier_semaphore()

    def greet_eta(s, c):
        pl.semaphore_signal(barrier, inc=1, device_id=(dep, lax.rem(eta + s, n_eta)), device_id_type=MESH)
        return c

    def greet_dep(s, c):
        pl.semaphore_signal(barrier, inc=1, device_id=(lax.rem(dep + s, n_dep), eta), device_id_type=MESH)
        return c

    loads = [
        pltpu.make_async_copy(src, dst, load_sem.at[n])
        for n, (src, dst) in enumerate(
            (
                (field_hbm, field),
                (fwd_hbm, tfwd),
                (efwd_hbm, efwd),
                (einv_hbm, einv),
                (weight_hbm, weight),
                (inv_hbm, tinv),
                (cotan_hbm, cotan),
            )
        )
    ]
    for copy in loads:
        copy.start()
    lax.fori_loop(1, n_eta, greet_eta, 0)
    lax.fori_loop(1, n_dep, greet_dep, 0)

    def eta_start(n, send, recv):
        def step(s, c):
            peer = lax.rem(eta + s, n_eta)
            pltpu.make_async_remote_copy(
                src_ref=send.at[pl.ds(pl.multiple_of(peer * 8, 8), 8)],
                dst_ref=recv.at[pl.ds(pl.multiple_of(eta * 8, 8), 8)],
                send_sem=send_sem.at[n],
                recv_sem=recv_sem.at[n],
                device_id=(dep, peer),
                device_id_type=MESH,
            ).start()
            return c

        lax.fori_loop(1, n_eta, step, 0)
        own = pl.ds(pl.multiple_of(eta * 8, 8), 8)
        recv[own, :] = send[own, :]

    def eta_wait(n, recv):
        rows = pl.ds(0, 8 * (n_eta - 1))
        pltpu.make_async_copy(recv.at[rows], recv.at[rows], recv_sem.at[n]).wait()

    def eta_sent(n, send):
        rows = pl.ds(0, 8 * (n_eta - 1))
        pltpu.make_async_copy(send.at[rows], send.at[rows], send_sem.at[n]).wait()

    def gather_start(n, axis, block, recv):
        me, count = (dep, n_dep) if axis == "depth" else (eta, n_eta)

        def step(s, c):
            peer = lax.rem(me + s, count)
            pltpu.make_async_remote_copy(
                src_ref=block,
                dst_ref=recv.at[me],
                send_sem=send_sem.at[n],
                recv_sem=recv_sem.at[n],
                device_id=(peer, eta) if axis == "depth" else (dep, peer),
                device_id_type=MESH,
            ).start()
            return c

        lax.fori_loop(1, count, step, 0)
        recv[me] = block[...]

    def blocks_wait(sem, recv, count):
        some = pl.ds(0, count - 1)
        pltpu.make_async_copy(recv.at[some], recv.at[some], sem).wait()

    def phi_forward(x, send):
        spectra = nt(tfwd[...], eta_order(x))
        for q in range(4):
            for hi in range(2):
                send[pl.ds(q * 2 + hi, n_eta, stride=8), :] = spectra[
                    q * n_eta : (q + 1) * n_eta, hi * 128 : (hi + 1) * 128
                ]

    def eta_forward(recv):
        xt = recv[...].T.astype(BF16)
        half = 8 * n_eta
        return nn(xt[0:64], efwd[0:half, :]) + nn(xt[64:128], efwd[half:, :])

    def eta_inverse(real, imag, send):
        v = jnp.concatenate([real, imag], axis=1).astype(BF16)
        zero = jnp.zeros_like(v)
        both = jnp.concatenate(
            [jnp.concatenate([v, zero], axis=1), jnp.concatenate([zero, v], axis=1)], axis=0
        )
        send[...] = nt(einv[...], both)

    def phi_inverse_lhs(recv):
        halves = []
        for hi in range(2):
            rows = [recv[pl.ds(q * 2 + hi, n_eta, stride=8), :] for q in range(4)]
            halves.append(jnp.concatenate(rows, axis=0).T)
        w_all[...] = cell_order(jnp.concatenate(halves, axis=0)).astype(BF16)

    def tile_rows(x):
        return jnp.concatenate([x] * 4, axis=0)

    spread_in = (
        lax.broadcasted_iota(jnp.int32, (64, 256), 0) == lax.rem(lax.broadcasted_iota(jnp.int32, (64, 256), 1), 64)
    ).astype(F32).astype(BF16)
    spread_out = (
        lax.broadcasted_iota(jnp.int32, (32, 128), 0) == lax.rem(lax.broadcasted_iota(jnp.int32, (32, 128), 1), 32)
    ).astype(F32).astype(BF16)
    in_tiled = tile_rows(nn(mlp_in[...], spread_in))
    keep = (
        lax.broadcasted_iota(jnp.int32, (128, 256), 0) // 32 == lax.broadcasted_iota(jnp.int32, (128, 256), 1) // 64
    )
    down = jnp.where(keep, in_tiled, 0.0)
    m_down[...] = down.astype(BF16)
    m_up[...] = down.T.astype(BF16)
    out_tiled = tile_rows(nn(mlp_out[...], spread_out))
    keep_out = (
        lax.broadcasted_iota(jnp.int32, (256, 128), 0) // 64 == lax.broadcasted_iota(jnp.int32, (256, 128), 1) // 32
    )
    outm = jnp.where(keep_out, out_tiled, 0.0)
    m_out[...] = outm.astype(BF16)
    m_outt[...] = outm.T.astype(BF16)
    diagonal = lax.broadcasted_iota(jnp.int32, (64, 64), 0) == lax.broadcasted_iota(jnp.int32, (64, 64), 1)
    column = jnp.sum(jnp.where(diagonal, mlp_bias[...], 0.0), axis=1, keepdims=True)
    bias_col[...] = jnp.broadcast_to(tile_rows(column), (256, 128))

    loads[0].wait()
    loads[1].wait()
    phi_forward(field[...], sends.at[0])
    pl.semaphore_wait(barrier, n_eta + n_dep - 2)
    eta_start(0, sends.at[0], recvs.at[0])

    def mlp_forward(g):
        def body(i, c):
            cols = pl.ds(pl.multiple_of(i * chunk, chunk), chunk)
            pre = nn(m_up[...], field[g * 128 : (g + 1) * 128, cols])
            pre = pre + jnp.concatenate([bias_col[...]] * (chunk // 128), axis=1)
            cdf, density = cdf_and_density(pre)
            hidden = (pre * cdf).astype(BF16)
            hid[g * 256 : (g + 1) * 256, cols] = hidden
            slope[g * 256 : (g + 1) * 256, cols] = (cdf + pre * density).astype(BF16)
            part[g * 128 : (g + 1) * 128, cols] = nn(m_outt[...], hidden)
            return c

        lax.fori_loop(0, n_chunks, body, 0)

    loads[4].wait()
    for ri in range(2):
        rt[ri] = weight[ri * 128 : (ri + 1) * 128, :].astype(F32).T
    mlp_forward(0)

    loads[2].wait()
    loads[3].wait()
    eta_wait(0, recvs.at[0])
    zx = eta_forward(recvs.at[0])
    for ri in range(2):
        zbuf[ri] = zx[:, ri * 128 : (ri + 1) * 128]
    dsend_x = zx

    def mix(table, sign):
        real = [jnp.zeros((32, 128), F32) for _ in range(2)]
        imag = [jnp.zeros((32, 128), F32) for _ in range(2)]
        for c in range(32):
            wr = table[0, c * 32 : (c + 1) * 32, :]
            wi = table[1, c * 32 : (c + 1) * 32, :]
            for d in range(2):
                zr = zbuf[0, d * 32 + c : d * 32 + c + 1, :]
                zi = zbuf[1, d * 32 + c : d * 32 + c + 1, :]
                real[d] = real[d] + (zr * wr - sign * (zi * wi))
                imag[d] = imag[d] + (zi * wr + sign * (zr * wi))
        return jnp.concatenate(real, axis=0), jnp.concatenate(imag, axis=0)

    vr, vi = mix(rt, 1.0)
    eta_inverse(vr, vi, sends.at[1])
    eta_start(1, sends.at[1], recvs.at[1])

    dsend[:, :, 0:64] = dsend_x.T.reshape(4, 64, 64)
    mlp_forward(1)
    for ri in range(2):
        for o in range(32):
            rt2[ri, o * 32 : (o + 1) * 32, :] = rt[ri, pl.ds(o, 32, stride=32), :]

    loads[5].wait()
    loads[6].wait()
    eta_wait(1, recvs.at[1])
    phi_inverse_lhs(recvs.at[1])

    def pre_body(i, c):
        cols = pl.ds(pl.multiple_of(i * chunk, chunk), chunk)
        pre = nn(w_all[...], tinv[:, cols]) + part[:, cols]
        cdf, density = cdf_and_density(pre)
        gpre[:, cols] = (cotan[:, cols].astype(F32) * (cdf + pre * density)).astype(BF16)
        return c

    lax.fori_loop(0, n_chunks, pre_body, 0)
    phi_forward(gpre[...], sends.at[2])
    eta_start(2, sends.at[2], recvs.at[2])

    def mlp_backward(g):
        def body(i, c):
            cols = pl.ds(pl.multiple_of(i * chunk, chunk), chunk)
            grad = nn(m_out[...], gpre[g * 128 : (g + 1) * 128, cols])
            grad = (grad * slope[g * 256 : (g + 1) * 256, cols].astype(F32)).astype(BF16)
            slope[g * 256 : (g + 1) * 256, cols] = grad
            rows = slice(g * 128, (g + 1) * 128)
            part[rows, cols] = cotan[rows, cols].astype(F32) + nn(m_down[...], grad)
            return c

        lax.fori_loop(0, n_chunks, body, 0)

    lane64 = lax.broadcasted_iota(jnp.int32, (64, 128), 1)
    lane32 = lax.broadcasted_iota(jnp.int32, (32, 128), 1)
    lane8 = lax.broadcasted_iota(jnp.int32, (8, 128), 1)
    sum_out = jnp.zeros((64, 128), F32)
    sum_in = jnp.zeros((32, 128), F32)
    sum_bias = jnp.zeros((8, 128), F32)
    ones = jnp.ones((8, n_phi), BF16)
    for g in range(2):
        mlp_backward(g)
        hgb = slope[g * 256 : (g + 1) * 256, :]
        by_in = nt(field[g * 128 : (g + 1) * 128, :], hgb)
        by_out = nt(hid[g * 256 : (g + 1) * 256, :], gpre[g * 128 : (g + 1) * 128, :])
        by_bias = nt(ones, hgb)
        for a in range(4):
            tile = by_in[a * 32 : (a + 1) * 32, (a // 2) * 128 : (a // 2 + 1) * 128]
            sum_in = sum_in + (pltpu.roll(tile, 64, 1) if a % 2 else tile)
            tile = by_out[a * 64 : (a + 1) * 64, :]
            turn = (64 - 32 * a) % 128
            sum_out = sum_out + (pltpu.roll(tile, turn, 1) if turn else tile)
            tile = by_bias[:, (a // 2) * 128 : (a // 2 + 1) * 128]
            sum_bias = sum_bias + (pltpu.roll(tile, 64, 1) if a % 2 else tile)
    total = jnp.where((lane64 >= 64) & (lane64 < 96), sum_out, 0.0)
    low = jnp.concatenate(
        [
            jnp.where(lane32 < 64, sum_in, 0.0),
            jnp.where(lane8 < 64, sum_bias, 0.0),
            jnp.zeros((24, 128), F32),
        ],
        axis=0,
    )
    asend[...] = (total + low).reshape(asend.shape)

    def scatter_step(s, c):
        peer = lax.rem(dep + s, n_dep)
        pltpu.make_async_remote_copy(
            src_ref=asend.at[peer],
            dst_ref=arecv.at[dep],
            send_sem=send_sem.at[4],
            recv_sem=recv_sem.at[4],
            device_id=(peer, eta),
            device_id_type=MESH,
        ).start()
        return c

    lax.fori_loop(1, n_dep, scatter_step, 0)
    arecv[dep] = asend[dep]

    eta_wait(2, recvs.at[2])
    zg = eta_forward(recvs.at[2])
    for ri in range(2):
        zbuf[ri] = zg[:, ri * 128 : (ri + 1) * 128]
    br, bi = mix(rt2, -1.0)
    eta_inverse(br, bi, sends.at[3])
    eta_start(3, sends.at[3], recvs.at[3])

    dsend[:, :, 64:128] = zg.T.reshape(4, 64, 64)
    mb = drecv.shape[2]

    def depth_step(s, c):
        peer = lax.rem(dep + s, n_dep)
        pltpu.make_async_remote_copy(
            src_ref=dsend.at[:, pl.ds(pl.multiple_of(peer * mb, mb), mb), :],
            dst_ref=drecv.at[dep],
            send_sem=send_sem.at[5],
            recv_sem=recv_sem.at[5],
            device_id=(peer, eta),
            device_id_type=MESH,
        ).start()
        return c

    lax.fori_loop(1, n_dep, depth_step, 0)
    drecv[dep] = dsend[:, pl.ds(pl.multiple_of(dep * mb, mb), mb), :]

    blocks_wait(recv_sem.at[4], arecv, n_dep)
    mine = arecv[0]
    for i in range(1, n_dep):
        mine = mine + arecv[i]
    bsend[...] = mine
    gather_start(6, "eta", bsend, brecv)

    blocks_wait(recv_sem.at[5], drecv, n_dep)
    got = drecv[...].reshape(256, 128)
    lane = lax.broadcasted_iota(jnp.int32, (256, 128), 1)
    row_c = lax.rem(lax.broadcasted_iota(jnp.int32, (128, 1024), 0), 32)
    repeat = (row_c == lax.broadcasted_iota(jnp.int32, (128, 1024), 1) // 32).astype(F32).astype(BF16)
    row_o = lax.rem(lax.broadcasted_iota(jnp.int32, (128, 128), 0), 32)
    tiled = (row_o == lax.rem(lax.broadcasted_iota(jnp.int32, (128, 128), 1), 32)).astype(F32).astype(BF16)
    for d in range(2):
        xexp[d] = nn(jnp.where(lane // 32 == d, got, 0.0).astype(BF16), repeat)
        gexp[d] = nn(jnp.where(lane // 32 == 2 + d, got, 0.0).astype(BF16), tiled)
    for kk in range(2):
        for t in range(8):
            lanes = slice(t * 128, (t + 1) * 128)
            real = jnp.zeros((mb, 128), F32)
            imag = jnp.zeros((mb, 128), F32)
            for i in range(n_dep):
                r0 = (i * 4 + kk) * mb
                r1 = (i * 4 + 2 + kk) * mb
                for d in range(2):
                    xr = xexp[d, r0 : r0 + mb, lanes]
                    xi = xexp[d, r1 : r1 + mb, lanes]
                    gr = gexp[d, r0 : r0 + mb, :]
                    gi = gexp[d, r1 : r1 + mb, :]
                    real = real + (xr * gr + xi * gi)
                    imag = imag + (xr * gi - xi * gr)
            gspec[0, kk, :, lanes] = real * factor
            gspec[1, kk, :, lanes] = imag * factor

    blocks_wait(recv_sem.at[6], brecv, n_eta)
    mine = brecv[0]
    for i in range(1, n_eta):
        mine = mine + brecv[i]
    csend[...] = mine * norm
    gather_start(7, "depth", csend, crecv)

    eta_wait(3, recvs.at[3])
    phi_inverse_lhs(recvs.at[3])

    outs = []
    for i in range(n_chunks):
        cols = pl.ds(i * chunk, chunk)
        part[:, cols] = part[:, cols] + nn(w_all[...], tinv[:, cols])
        copy = pltpu.make_async_copy(part.at[:, cols], gin_hbm.at[:, cols], out_sem.at[i])
        copy.start()
        outs.append(copy)

    blocks_wait(recv_sem.at[7], crecv, n_dep)
    sums = crecv[...].reshape(64, 128)
    out_in[...] = sums[0:32, 0:64]
    out_out[...] = pltpu.roll(sums, 64, 1)[:, 0:32]
    out_bias[...] = sums[32:33, 0:64]

    for n in range(4):
        eta_sent(n, sends.at[n])
    blocks_wait(send_sem.at[4], arecv, n_dep)
    blocks_wait(send_sem.at[5], drecv, n_dep)
    blocks_wait(send_sem.at[6], brecv, n_eta)
    blocks_wait(send_sem.at[7], crecv, n_dep)
    for copy in outs:
        copy.wait()


def local(n_dep, n_eta, field_in, grad_out, spectral_weight, mlp_in, mlp_bias, mlp_out):
    layers, cells, chans, n_phi = field_in.shape
    owned, n_modes = spectral_weight.shape[1:3]
    n_cells = cells * n_eta
    assert (layers, cells, chans, owned, n_modes) == (2, 4, 32, 2, 64)
    fwd, inv = phi_table(n_phi, owned * n_eta)
    efwd, einv = eta_tables(n_cells, n_modes, n_eta)
    rows = layers * cells * chans
    mb = n_modes // n_dep
    chunk = min(256, n_phi)
    factor = math.sqrt(n_phi * n_cells / (owned * n_eta * n_modes))
    norm = 1.0 / math.sqrt(layers * n_dep * n_cells * n_phi)
    vmem = pl.BlockSpec(memory_space=pltpu.VMEM)
    hbm = pl.BlockSpec(memory_space=pl.ANY)
    part = 64 // n_dep
    scratch = [
        pltpu.VMEM((rows, n_phi), BF16),
        pltpu.VMEM((rows, n_phi), BF16),
        pltpu.VMEM((4 * n_modes, 1024), BF16),
        pltpu.VMEM(fwd.shape, BF16),
        pltpu.VMEM(inv.shape, BF16),
        pltpu.VMEM(efwd.shape, BF16),
        pltpu.VMEM(einv.shape, BF16),
        pltpu.VMEM((2 * rows, n_phi), BF16),
        pltpu.VMEM((2 * rows, n_phi), BF16),
        pltpu.VMEM((rows, n_phi), F32),
        pltpu.VMEM((rows, n_phi), BF16),
        pltpu.VMEM((rows, 4 * n_eta), BF16),
        pltpu.VMEM((256, 128), BF16),
        pltpu.VMEM((128, 256), BF16),
        pltpu.VMEM((128, 256), BF16),
        pltpu.VMEM((256, 128), BF16),
        pltpu.VMEM((256, 128), F32),
        pltpu.VMEM((2, 1024, 128), F32),
        pltpu.VMEM((2, 1024, 128), F32),
        pltpu.VMEM((2, 64, 128), F32),
        pltpu.VMEM((8, 128), F32),
        pltpu.VMEM((4, 8 * n_eta, 128), F32),
        pltpu.VMEM((4, 8 * n_eta, 128), F32),
        pltpu.VMEM((4, 64, 128), F32),
        pltpu.VMEM((n_dep, 4, mb, 128), F32),
        pltpu.VMEM((2, 256, 1024), F32),
        pltpu.VMEM((2, 256, 128), F32),
        pltpu.VMEM((n_dep, part, 128), F32),
        pltpu.VMEM((n_dep, part, 128), F32),
        pltpu.VMEM((part, 128), F32),
        pltpu.VMEM((n_eta, part, 128), F32),
        pltpu.VMEM((part, 128), F32),
        pltpu.VMEM((n_dep, part, 128), F32),
        pltpu.SemaphoreType.DMA((7,)),
        pltpu.SemaphoreType.DMA((n_phi // chunk,)),
        pltpu.SemaphoreType.DMA((8,)),
        pltpu.SemaphoreType.DMA((8,)),
    ]
    gin, gspec, g_in, g_out, g_bias = pl.pallas_call(
        functools.partial(kernel, n_dep, n_eta, chunk, factor, norm),
        out_shape=(
            jax.ShapeDtypeStruct((rows, n_phi), F32),
            jax.ShapeDtypeStruct((2, 2, mb, 1024), F32),
            jax.ShapeDtypeStruct((32, 64), F32),
            jax.ShapeDtypeStruct((64, 32), F32),
            jax.ShapeDtypeStruct((1, 64), F32),
        ),
        in_specs=[hbm, hbm, hbm, vmem, vmem, vmem, hbm, hbm, hbm, hbm],
        out_specs=(hbm, vmem, vmem, vmem, vmem),
        scratch_shapes=scratch,
        compiler_params=pltpu.CompilerParams(
            collective_id=0, has_side_effects=True, vmem_limit_bytes=48 * 1024 * 1024
        ),
    )(
        field_in.reshape(rows, n_phi),
        grad_out.reshape(rows, n_phi),
        spectral_weight.reshape(4 * n_modes, 1024),
        mlp_in,
        mlp_bias.reshape(1, 64),
        mlp_out,
        jnp.asarray(fwd),
        jnp.asarray(inv),
        jnp.asarray(efwd),
        jnp.asarray(einv),
    )
    return gin.reshape(layers, cells, chans, n_phi), gspec, g_in, g_out, g_bias.reshape(64)


def solution(mesh):
    return jax.shard_map(
        functools.partial(local, mesh.shape["depth"], mesh.shape["eta"]),
        mesh=mesh,
        in_specs=(
            P("depth", "eta", None, None),
            P("depth", "eta", None, None),
            P(None, "eta", None, None),
            P(),
            P(),
            P(),
        ),
        out_specs=(P("depth", "eta", None, None), P(None, "eta", "depth", None), P(), P(), P()),
        check_vma=False,
    )
```

time: 935 us -> 66.4 us (0.07)
  the two profiles are of different devices: /device:TPU:64 before, /device:TPU:1 now
where the time goes in v1:
time: 66.4 us; the launch traced here: 65.9 us
  Pallas kernels  50.1 us (75%)
  local copies, waits for them, and re-layouts  15.2 us (23%)
    pallas_call x1, Pallas kernels, local(): pl.pallas_call(functools.partial(kernel, n_dep, n_eta, chunk, factor, nor...  50.1 us
    unnamed x24, local copies, waits for them, and re-layouts  15.2 us

profile of v1, /device:TPU:1, one launch (start us, length us, event | category | flops | bytes accessed | tf_op | source)
XLA Modules:
  0.0 65.9 jit_solution(8278347627779691145)
XLA Ops:
  0.6 0.8 %copy.15.mlp_out = bf16[64,32]{1,0:T(8,128)(2,1)S(1)} copy(bf16[64,32]{0,1:T(8,128)(2,1)} %param.15) | data formatting | bytes 8192 | tf_op args[5]
  1.4 0.0 copy-start
  1.4 1.2 %copy-done = bf16[2,4,32,2048]{3,2,1,0:T(8,128)(2,1)S(1)} copy-done((bf16[2,4,32,2048]{3,2,1,0:T(8,128)(2,1)S(1)}, bf16[2,4,32,2048]{3,2,1,0:T(8,128)(2,1)}, u32[]{:S(2)}) %copy-start) | copy-done | bytes 1048600
  2.6 0.0 copy-start.1
  2.7 1.2 %copy-done.1 = bf16[2,4,32,2048]{3,2,1,0:T(8,128)(2,1)S(1)} copy-done((bf16[2,4,32,2048]{3,2,1,0:T(8,128)(2,1)S(1)}, bf16[2,4,32,2048]{3,2,1,0:T(8,128)(2,1)}, u32[]{:S(2)}) %copy-start.1) | copy-done | bytes 1048600
  3.9 1.0 %copy-done.2 = bf16[2,2,64,1024]{3,2,1,0:T(8,128)(2,1)S(1)} copy-done((bf16[2,2,64,1024]{3,2,1,0:T(8,128)(2,1)S(1)}, bf16[2,2,64,1024]{3,2,1,0:T(8,128)(2,1)}, u32[]{:S(2)}) %copy-start.2) | copy-done | bytes 524312
  4.9 0.0 copy-start.3
  4.9 1.0 %copy-done.3 = bf16[128,2048]{1,0:T(8,128)(2,1)S(1)} copy-done((bf16[128,2048]{1,0:T(8,128)(2,1)S(1)}, bf16[128,2048]{1,0:T(8,128)(2,1)}, u32[]{:S(2)}) %copy-start.3) | copy-done | bytes 524312
  6.0 0.0 copy-start.4
  6.0 1.0 %copy-done.4 = bf16[128,2048]{1,0:T(8,128)(2,1)S(1)} copy-done((bf16[128,2048]{1,0:T(8,128)(2,1)S(1)}, bf16[128,2048]{1,0:T(8,128)(2,1)}, u32[]{:S(2)}) %copy-start.4) | copy-done | bytes 524312
  7.0 0.0 copy-start.5
  7.0 0.9 %copy-done.5 = bf16[256,512]{1,0:T(8,128)(2,1)S(1)} copy-done((bf16[256,512]{1,0:T(8,128)(2,1)S(1)}, bf16[256,512]{1,0:T(8,128)(2,1)}, u32[]{:S(2)}) %copy-start.5) | copy-done | bytes 262168
  8.0 0.0 copy-start.6
  8.0 0.9 %copy-done.6 = bf16[512,256]{1,0:T(8,128)(2,1)S(1)} copy-done((bf16[512,256]{1,0:T(8,128)(2,1)S(1)}, bf16[512,256]{1,0:T(8,128)(2,1)}, u32[]{:S(2)}) %copy-start.6) | copy-done | bytes 262168
  8.9 0.0 copy-start.7
  8.9 0.7 %copy-done.7 = bf16[32,64]{1,0:T(8,128)(2,1)S(1)} copy-done((bf16[32,64]{1,0:T(8,128)(2,1)S(1)}, bf16[32,64]{1,0:T(8,128)(2,1)}, u32[]{:S(2)}) %copy-start.7) | copy-done | bytes 4120
  9.6 0.0 copy-start.8
  9.6 0.7 copy-done.8
  10.3 50.1 %shard_map.137 = (f32[256,2048]{1,0:T(8,128)}, f32[2,2,8,1024]{3,2,1,0:T(8,128)S(1)}, f32[32,64]{1,0:T(8,128)S(1)}, f32[64,32]{1,0:T(8,128)S(1)}, f32[1,64]{1,0:T(1,128)S(1)}) custom-call(bf16[256,2048]{1,0:T(8,128)(2,1)S(1)} %bitcast.6, bf16[256,2048]{1,0:T(8,128)(2,1)S(1)} %bitcast.7, bf16[256,1024]{1,0:T(8,128)(2,1)S(1)} %bitcast.8, ...), custom_call_target="tpu_custom_call" | custom-call | tf_op jit(solution)/shard_map/pallas_call | solution.py:553
  60.3 0.7 %copy.16 = f32[64,32]{0,1:T(8,128)} copy(f32[64,32]{1,0:T(8,128)S(1)} %get-tuple-element.18) | data formatting | bytes 16384
  61.0 3.1 %copy.21 = f32[2,4,32,2048]{3,2,1,0:T(8,128)} copy(f32[2,4,32,2048]{3,2,1,0:T(8,128)} %bitcast.11) | data formatting | bytes 4194304
  64.2 0.7 copy.22
  64.8 0.6 copy.23
  65.4 0.5 copy.24
  (1 shorter events, 0.0 us)
Async XLA Ops:
  1.4 1.2 %copy-start = (bf16[2,4,32,2048]{3,2,1,0:T(8,128)(2,1)S(1)}, bf16[2,4,32,2048]{3,2,1,0:T(8,128)(2,1)}, u32[]{:S(2)}) copy-start(bf16[2,4,32,2048]{3,2,1,0:T(8,128)(2,1)} %param.10) | copy-start | bytes 3145732
  2.6 1.2 %copy-start.1 = (bf16[2,4,32,2048]{3,2,1,0:T(8,128)(2,1)S(1)}, bf16[2,4,32,2048]{3,2,1,0:T(8,128)(2,1)}, u32[]{:S(2)}) copy-start(bf16[2,4,32,2048]{3,2,1,0:T(8,128)(2,1)} %param.11) | copy-start | bytes 3145732
  3.9 1.0 %copy-start.2 = (bf16[2,2,64,1024]{3,2,1,0:T(8,128)(2,1)S(1)}, bf16[2,2,64,1024]{3,2,1,0:T(8,128)(2,1)}, u32[]{:S(2)}) copy-start(bf16[2,2,64,1024]{3,2,1,0:T(8,128)(2,1)} %param.12) | copy-start | bytes 1572868
  4.9 1.0 %copy-start.3 = (bf16[128,2048]{1,0:T(8,128)(2,1)S(1)}, bf16[128,2048]{1,0:T(8,128)(2,1)}, u32[]{:S(2)}) copy-start(bf16[128,2048]{1,0:T(8,128)(2,1)} %constant.9.clone.inv_hbm) | copy-start | bytes 1572868
  6.0 1.0 %copy-start.4 = (bf16[128,2048]{1,0:T(8,128)(2,1)S(1)}, bf16[128,2048]{1,0:T(8,128)(2,1)}, u32[]{:S(2)}) copy-start(bf16[128,2048]{1,0:T(8,128)(2,1)} %constant.8.clone.fwd_hbm) | copy-start | bytes 1572868
  7.0 0.9 %copy-start.5 = (bf16[256,512]{1,0:T(8,128)(2,1)S(1)}, bf16[256,512]{1,0:T(8,128)(2,1)}, u32[]{:S(2)}) copy-start(bf16[256,512]{1,0:T(8,128)(2,1)} %constant.11.clone.einv_hbm) | copy-start | bytes 786436
  8.0 0.9 %copy-start.6 = (bf16[512,256]{1,0:T(8,128)(2,1)S(1)}, bf16[512,256]{1,0:T(8,128)(2,1)}, u32[]{:S(2)}) copy-start(bf16[512,256]{1,0:T(8,128)(2,1)} %constant.10.clone.efwd_hbm) | copy-start | bytes 786436
  8.9 0.7 %copy-start.7 = (bf16[32,64]{1,0:T(8,128)(2,1)S(1)}, bf16[32,64]{1,0:T(8,128)(2,1)}, u32[]{:S(2)}) copy-start(bf16[32,64]{1,0:T(8,128)(2,1)} %mlp_in.1) | copy-start | bytes 12292
  9.6 0.7 copy-start.8

commit v2 on v1

--- a/solution.py
+++ b/solution.py
@@ -51,6 +51,20 @@
     return bf(fwd), bf(inv)
 
 
+def far_first(n_eta):
+    if n_eta != 32:
+        return [(s,) for s in range(1, n_eta)]
+    steps = [(x, z, y) for x in range(4) for z in range(2) for y in range(4)]
+    return sorted(steps[1:], key=lambda s: -(min(s[0], 4 - s[0]) + s[1] + min(s[2], 4 - s[2])))
+
+
+def eta_peer(eta, n_eta, step):
+    if len(step) == 1:
+        return lax.rem(eta + step[0], n_eta)
+    x, z, y = eta // 8, lax.rem(eta // 4, 2), lax.rem(eta, 4)
+    return lax.rem(x + step[0], 4) * 8 + lax.rem(z + step[1], 2) * 4 + lax.rem(y + step[2], 4)
+
+
 def nn(a, b):
     return lax.dot_general(a, b, (((1,), (0,)), ((), ())), preferred_element_type=F32)
 
@@ -84,14 +98,14 @@
     field_hbm,
     cotan_hbm,
     weight_hbm,
-    mlp_in,
-    mlp_bias,
-    mlp_out,
+    mlp_in_hbm,
+    mlp_bias_hbm,
+    mlp_outt_hbm,
     fwd_hbm,
     inv_hbm,
     efwd_hbm,
     einv_hbm,
-    gin_hbm,
+    part,
     gspec,
     out_in,
     out_out,
@@ -105,7 +119,6 @@
     einv,
     hid,
     slope,
-    part,
     gpre,
     w_all,
     m_up,
@@ -116,7 +129,9 @@
     rt,
     rt2,
     zbuf,
-    vsend,
+    mlp_in,
+    mlp_bias,
+    mlp_outt,
     sends,
     recvs,
     dsend,
@@ -130,7 +145,6 @@
     csend,
     crecv,
     load_sem,
-    out_sem,
     send_sem,
     recv_sem,
 ):
@@ -141,13 +155,12 @@
 
     barrier = pltpu.get_barrier_semaphore()
 
-    def greet_eta(s, c):
-        pl.semaphore_signal(barrier, inc=1, device_id=(dep, lax.rem(eta + s, n_eta)), device_id_type=MESH)
-        return c
-
-    def greet_dep(s, c):
-        pl.semaphore_signal(barrier, inc=1, device_id=(lax.rem(dep + s, n_dep), eta), device_id_type=MESH)
-        return c
+    eta_peers = [eta_peer(eta, n_eta, step) for step in far_first(n_eta)]
+    dep_peers = [lax.rem(dep + s, n_dep) for s in range(1, n_dep)]
+    for peer in eta_peers:
+        pl.semaphore_signal(barrier, inc=1, device_id=(dep, peer), device_id_type=MESH)
+    for peer in dep_peers:
+        pl.semaphore_signal(barrier, inc=1, device_id=(peer, eta), device_id_type=MESH)
 
     loads = [
         pltpu.make_async_copy(src, dst, load_sem.at[n])
@@ -160,17 +173,17 @@
                 (weight_hbm, weight),
                 (inv_hbm, tinv),
                 (cotan_hbm, cotan),
+                (mlp_in_hbm, mlp_in),
+                (mlp_bias_hbm, mlp_bias),
+                (mlp_outt_hbm, mlp_outt),
             )
         )
     ]
     for copy in loads:
         copy.start()
-    lax.fori_loop(1, n_eta, greet_eta, 0)
-    lax.fori_loop(1, n_dep, greet_dep, 0)
 
     def eta_start(n, send, recv):
-        def step(s, c):
-            peer = lax.rem(eta + s, n_eta)
+        for peer in eta_peers:
             pltpu.make_async_remote_copy(
                 src_ref=send.at[pl.ds(pl.multiple_of(peer * 8, 8), 8)],
                 dst_ref=recv.at[pl.ds(pl.multiple_of(eta * 8, 8), 8)],
@@ -179,9 +192,6 @@
                 device_id=(dep, peer),
                 device_id_type=MESH,
             ).start()
-            return c
-
-        lax.fori_loop(1, n_eta, step, 0)
         own = pl.ds(pl.multiple_of(eta * 8, 8), 8)
         recv[own, :] = send[own, :]
 
@@ -194,10 +204,8 @@
         pltpu.make_async_copy(send.at[rows], send.at[rows], send_sem.at[n]).wait()
 
     def gather_start(n, axis, block, recv):
-        me, count = (dep, n_dep) if axis == "depth" else (eta, n_eta)
-
-        def step(s, c):
-            peer = lax.rem(me + s, count)
+        me, peers = (dep, dep_peers) if axis == "depth" else (eta, eta_peers)
+        for peer in peers:
             pltpu.make_async_remote_copy(
                 src_ref=block,
                 dst_ref=recv.at[me],
@@ -206,9 +214,6 @@
                 device_id=(peer, eta) if axis == "depth" else (dep, peer),
                 device_id_type=MESH,
             ).start()
-            return c
-
-        lax.fori_loop(1, count, step, 0)
         recv[me] = block[...]
 
     def blocks_wait(sem, recv, count):
@@ -243,38 +248,31 @@
             halves.append(jnp.concatenate(rows, axis=0).T)
         w_all[...] = cell_order(jnp.concatenate(halves, axis=0)).astype(BF16)
 
-    def tile_rows(x):
-        return jnp.concatenate([x] * 4, axis=0)
-
-    spread_in = (
-        lax.broadcasted_iota(jnp.int32, (64, 256), 0) == lax.rem(lax.broadcasted_iota(jnp.int32, (64, 256), 1), 64)
-    ).astype(F32).astype(BF16)
-    spread_out = (
-        lax.broadcasted_iota(jnp.int32, (32, 128), 0) == lax.rem(lax.broadcasted_iota(jnp.int32, (32, 128), 1), 32)
-    ).astype(F32).astype(BF16)
-    in_tiled = tile_rows(nn(mlp_in[...], spread_in))
-    keep = (
-        lax.broadcasted_iota(jnp.int32, (128, 256), 0) // 32 == lax.broadcasted_iota(jnp.int32, (128, 256), 1) // 64
-    )
-    down = jnp.where(keep, in_tiled, 0.0)
-    m_down[...] = down.astype(BF16)
-    m_up[...] = down.T.astype(BF16)
-    out_tiled = tile_rows(nn(mlp_out[...], spread_out))
-    keep_out = (
-        lax.broadcasted_iota(jnp.int32, (256, 128), 0) // 64 == lax.broadcasted_iota(jnp.int32, (256, 128), 1) // 32
-    )
-    outm = jnp.where(keep_out, out_tiled, 0.0)
-    m_out[...] = outm.astype(BF16)
-    m_outt[...] = outm.T.astype(BF16)
-    diagonal = lax.broadcasted_iota(jnp.int32, (64, 64), 0) == lax.broadcasted_iota(jnp.int32, (64, 64), 1)
-    column = jnp.sum(jnp.where(diagonal, mlp_bias[...], 0.0), axis=1, keepdims=True)
-    bias_col[...] = jnp.broadcast_to(tile_rows(column), (256, 128))
-
     loads[0].wait()
     loads[1].wait()
     phi_forward(field[...], sends.at[0])
     pl.semaphore_wait(barrier, n_eta + n_dep - 2)
     eta_start(0, sends.at[0], recvs.at[0])
+
+    for copy in loads[7:]:
+        copy.wait()
+
+    def tile_rows(x):
+        return jnp.concatenate([x] * 4, axis=0)
+
+    spread = (
+        lax.broadcasted_iota(jnp.int32, (64, 256), 0) == lax.rem(lax.broadcasted_iota(jnp.int32, (64, 256), 1), 64)
+    ).astype(F32).astype(BF16)
+    keep = (
+        lax.broadcasted_iota(jnp.int32, (128, 256), 0) // 32 == lax.broadcasted_iota(jnp.int32, (128, 256), 1) // 64
+    )
+    for matrix, wide, tall in ((mlp_in, m_down, m_up), (mlp_outt, m_outt, m_out)):
+        four = jnp.where(keep, tile_rows(nn(matrix[...], spread)), 0.0)
+        wide[...] = four.astype(BF16)
+        tall[...] = four.T.astype(BF16)
+    diagonal = lax.broadcasted_iota(jnp.int32, (64, 64), 0) == lax.broadcasted_iota(jnp.int32, (64, 64), 1)
+    column = jnp.sum(jnp.where(diagonal, mlp_bias[...], 0.0), axis=1, keepdims=True)
+    bias_col[...] = jnp.broadcast_to(tile_rows(column), (256, 128))
 
     def mlp_forward(g):
         def body(i, c):
@@ -346,48 +344,51 @@
         def body(i, c):
             cols = pl.ds(pl.multiple_of(i * chunk, chunk), chunk)
             grad = nn(m_out[...], gpre[g * 128 : (g + 1) * 128, cols])
-            grad = (grad * slope[g * 256 : (g + 1) * 256, cols].astype(F32)).astype(BF16)
-            slope[g * 256 : (g + 1) * 256, cols] = grad
+            slope[g * 256 : (g + 1) * 256, cols] = (
+                grad * slope[g * 256 : (g + 1) * 256, cols].astype(F32)
+            ).astype(BF16)
+            return c
+
+        lax.fori_loop(0, n_chunks, body, 0)
+
+    def mlp_to_input(g):
+        def body(i, c):
+            cols = pl.ds(pl.multiple_of(i * chunk, chunk), chunk)
             rows = slice(g * 128, (g + 1) * 128)
-            part[rows, cols] = cotan[rows, cols].astype(F32) + nn(m_down[...], grad)
+            part[rows, cols] = cotan[rows, cols].astype(F32) + nn(
+                m_down[...], slope[g * 256 : (g + 1) * 256, cols]
+            )
             return c
 
         lax.fori_loop(0, n_chunks, body, 0)
 
-    lane64 = lax.broadcasted_iota(jnp.int32, (64, 128), 1)
-    lane32 = lax.broadcasted_iota(jnp.int32, (32, 128), 1)
-    lane8 = lax.broadcasted_iota(jnp.int32, (8, 128), 1)
-    sum_out = jnp.zeros((64, 128), F32)
+    def fold(x):
+        rows = x.shape[0] // 4 if x.shape[0] > 8 else 0
+        acc = None
+        for a in range(4):
+            tile = x[a * rows : a * rows + (rows or 8), (a // 2) * 128 : (a // 2 + 1) * 128]
+            tile = pltpu.roll(tile, 64, 1) if a % 2 else tile
+            acc = tile if acc is None else acc + tile
+        return acc
+
     sum_in = jnp.zeros((32, 128), F32)
+    sum_out = jnp.zeros((32, 128), F32)
     sum_bias = jnp.zeros((8, 128), F32)
     ones = jnp.ones((8, n_phi), BF16)
     for g in range(2):
         mlp_backward(g)
-        hgb = slope[g * 256 : (g + 1) * 256, :]
-        by_in = nt(field[g * 128 : (g + 1) * 128, :], hgb)
-        by_out = nt(hid[g * 256 : (g + 1) * 256, :], gpre[g * 128 : (g + 1) * 128, :])
-        by_bias = nt(ones, hgb)
-        for a in range(4):
-            tile = by_in[a * 32 : (a + 1) * 32, (a // 2) * 128 : (a // 2 + 1) * 128]
-            sum_in = sum_in + (pltpu.roll(tile, 64, 1) if a % 2 else tile)
-            tile = by_out[a * 64 : (a + 1) * 64, :]
-            turn = (64 - 32 * a) % 128
-            sum_out = sum_out + (pltpu.roll(tile, turn, 1) if turn else tile)
-            tile = by_bias[:, (a // 2) * 128 : (a // 2 + 1) * 128]
-            sum_bias = sum_bias + (pltpu.roll(tile, 64, 1) if a % 2 else tile)
-    total = jnp.where((lane64 >= 64) & (lane64 < 96), sum_out, 0.0)
-    low = jnp.concatenate(
-        [
-            jnp.where(lane32 < 64, sum_in, 0.0),
-            jnp.where(lane8 < 64, sum_bias, 0.0),
-            jnp.zeros((24, 128), F32),
-        ],
+        grads = slope[g * 256 : (g + 1) * 256, :]
+        sum_in = sum_in + fold(nt(field[g * 128 : (g + 1) * 128, :], grads))
+        sum_out = sum_out + fold(nt(gpre[g * 128 : (g + 1) * 128, :], hid[g * 256 : (g + 1) * 256, :]))
+        sum_bias = sum_bias + fold(nt(ones, grads))
+    lane32 = lax.broadcasted_iota(jnp.int32, (32, 128), 1)
+    total = jnp.concatenate(
+        [jnp.where(lane32 < 64, sum_in, pltpu.roll(sum_out, 64, 1)), sum_bias, jnp.zeros((24, 128), F32)],
         axis=0,
     )
-    asend[...] = (total + low).reshape(asend.shape)
-
-    def scatter_step(s, c):
-        peer = lax.rem(dep + s, n_dep)
+    asend[...] = total.reshape(asend.shape)
+
+    for peer in dep_peers:
         pltpu.make_async_remote_copy(
             src_ref=asend.at[peer],
             dst_ref=arecv.at[dep],
@@ -396,9 +397,6 @@
             device_id=(peer, eta),
             device_id_type=MESH,
         ).start()
-        return c
-
-    lax.fori_loop(1, n_dep, scatter_step, 0)
     arecv[dep] = asend[dep]
 
     eta_wait(2, recvs.at[2])
@@ -412,8 +410,7 @@
     dsend[:, :, 64:128] = zg.T.reshape(4, 64, 64)
     mb = drecv.shape[2]
 
-    def depth_step(s, c):
-        peer = lax.rem(dep + s, n_dep)
+    for peer in dep_peers:
         pltpu.make_async_remote_copy(
             src_ref=dsend.at[:, pl.ds(pl.multiple_of(peer * mb, mb), mb), :],
             dst_ref=drecv.at[dep],
@@ -422,17 +419,17 @@
             device_id=(peer, eta),
             device_id_type=MESH,
         ).start()
-        return c
-
-    lax.fori_loop(1, n_dep, depth_step, 0)
     drecv[dep] = dsend[:, pl.ds(pl.multiple_of(dep * mb, mb), mb), :]
 
+    mlp_to_input(0)
     blocks_wait(recv_sem.at[4], arecv, n_dep)
     mine = arecv[0]
     for i in range(1, n_dep):
         mine = mine + arecv[i]
     bsend[...] = mine
     gather_start(6, "eta", bsend, brecv)
+
+    mlp_to_input(1)
 
     blocks_wait(recv_sem.at[5], drecv, n_dep)
     got = drecv[...].reshape(256, 128)
@@ -462,28 +459,26 @@
             gspec[0, kk, :, lanes] = real * factor
             gspec[1, kk, :, lanes] = imag * factor
 
+    eta_wait(3, recvs.at[3])
+    phi_inverse_lhs(recvs.at[3])
+
+    def gin_body(i, c):
+        cols = pl.ds(pl.multiple_of(i * chunk, chunk), chunk)
+        part[:, cols] = part[:, cols] + nn(w_all[...], tinv[:, cols])
+        return c
+
+    lax.fori_loop(0, n_chunks, gin_body, 0)
+
     blocks_wait(recv_sem.at[6], brecv, n_eta)
     mine = brecv[0]
     for i in range(1, n_eta):
         mine = mine + brecv[i]
     csend[...] = mine * norm
     gather_start(7, "depth", csend, crecv)
-
-    eta_wait(3, recvs.at[3])
-    phi_inverse_lhs(recvs.at[3])
-
-    outs = []
-    for i in range(n_chunks):
-        cols = pl.ds(i * chunk, chunk)
-        part[:, cols] = part[:, cols] + nn(w_all[...], tinv[:, cols])
-        copy = pltpu.make_async_copy(part.at[:, cols], gin_hbm.at[:, cols], out_sem.at[i])
-        copy.start()
-        outs.append(copy)
-
     blocks_wait(recv_sem.at[7], crecv, n_dep)
     sums = crecv[...].reshape(64, 128)
     out_in[...] = sums[0:32, 0:64]
-    out_out[...] = pltpu.roll(sums, 64, 1)[:, 0:32]
+    out_out[...] = pltpu.roll(sums[0:32, :], 64, 1)[:, 0:64]
     out_bias[...] = sums[32:33, 0:64]
 
     for n in range(4):
@@ -492,7 +487,14 @@
     blocks_wait(send_sem.at[5], drecv, n_dep)
     blocks_wait(send_sem.at[6], brecv, n_eta)
     blocks_wait(send_sem.at[7], crecv, n_dep)
-    for copy in outs:
+
+
+def write_out(*refs):
+    ins, outs, sem = refs[:5], refs[5:10], refs[10]
+    copies = [pltpu.make_async_copy(src, dst, sem.at[n]) for n, (src, dst) in enumerate(zip(ins, outs))]
+    for copy in copies:
+        copy.start()
+    for copy in copies:
         copy.wait()
 
 
@@ -509,7 +511,7 @@
     factor = math.sqrt(n_phi * n_cells / (owned * n_eta * n_modes))
     norm = 1.0 / math.sqrt(layers * n_dep * n_cells * n_phi)
     vmem = pl.BlockSpec(memory_space=pltpu.VMEM)
-    hbm = pl.BlockSpec(memory_space=pl.ANY)
+    hbm = pl.BlockSpec(memory_space=pltpu.HBM)
     part = 64 // n_dep
     scratch = [
         pltpu.VMEM((rows, n_phi), BF16),
@@ -521,7 +523,6 @@
         pltpu.VMEM(einv.shape, BF16),
         pltpu.VMEM((2 * rows, n_phi), BF16),
         pltpu.VMEM((2 * rows, n_phi), BF16),
-        pltpu.VMEM((rows, n_phi), F32),
         pltpu.VMEM((rows, n_phi), BF16),
         pltpu.VMEM((rows, 4 * n_eta), BF16),
         pltpu.VMEM((256, 128), BF16),
@@ -532,7 +533,9 @@
         pltpu.VMEM((2, 1024, 128), F32),
         pltpu.VMEM((2, 1024, 128), F32),
         pltpu.VMEM((2, 64, 128), F32),
-        pltpu.VMEM((8, 128), F32),
+        pltpu.VMEM((32, 64), BF16),
+        pltpu.VMEM((1, 64), F32),
+        pltpu.VMEM((32, 64), BF16),
         pltpu.VMEM((4, 8 * n_eta, 128), F32),
         pltpu.VMEM((4, 8 * n_eta, 128), F32),
         pltpu.VMEM((4, 64, 128), F32),
@@ -545,39 +548,41 @@
         pltpu.VMEM((n_eta, part, 128), F32),
         pltpu.VMEM((part, 128), F32),
         pltpu.VMEM((n_dep, part, 128), F32),
-        pltpu.SemaphoreType.DMA((7,)),
-        pltpu.SemaphoreType.DMA((n_phi // chunk,)),
+        pltpu.SemaphoreType.DMA((10,)),
         pltpu.SemaphoreType.DMA((8,)),
         pltpu.SemaphoreType.DMA((8,)),
     ]
-    gin, gspec, g_in, g_out, g_bias = pl.pallas_call(
-        functools.partial(kernel, n_dep, n_eta, chunk, factor, norm),
-        out_shape=(
-            jax.ShapeDtypeStruct((rows, n_phi), F32),
-            jax.ShapeDtypeStruct((2, 2, mb, 1024), F32),
-            jax.ShapeDtypeStruct((32, 64), F32),
-            jax.ShapeDtypeStruct((64, 32), F32),
-            jax.ShapeDtypeStruct((1, 64), F32),
-        ),
-        in_specs=[hbm, hbm, hbm, vmem, vmem, vmem, hbm, hbm, hbm, hbm],
-        out_specs=(hbm, vmem, vmem, vmem, vmem),
-        scratch_shapes=scratch,
-        compiler_params=pltpu.CompilerParams(
-            collective_id=0, has_side_effects=True, vmem_limit_bytes=48 * 1024 * 1024
-        ),
-    )(
+    sizes = ((rows, n_phi), (2, 2, mb, 1024), (32, 64), (32, 64), (1, 64))
+    operands = (
         field_in.reshape(rows, n_phi),
         grad_out.reshape(rows, n_phi),
         spectral_weight.reshape(4 * n_modes, 1024),
         mlp_in,
         mlp_bias.reshape(1, 64),
-        mlp_out,
+        mlp_out.T,
         jnp.asarray(fwd),
         jnp.asarray(inv),
         jnp.asarray(efwd),
         jnp.asarray(einv),
     )
-    return gin.reshape(layers, cells, chans, n_phi), gspec, g_in, g_out, g_bias.reshape(64)
+    results = pl.pallas_call(
+        functools.partial(kernel, n_dep, n_eta, chunk, factor, norm),
+        out_shape=tuple(pltpu.VMEM(size, F32) for size in sizes),
+        in_specs=[hbm] * 10,
+        out_specs=(vmem,) * 5,
+        scratch_shapes=scratch,
+        compiler_params=pltpu.CompilerParams(
+            collective_id=0, has_side_effects=True, vmem_limit_bytes=48 * 1024 * 1024
+        ),
+    )(*(pltpu.with_memory_space_constraint(x, pltpu.HBM) for x in operands))
+    gin, gspec, g_in, g_outt, g_bias = pl.pallas_call(
+        write_out,
+        out_shape=tuple(jax.ShapeDtypeStruct(size, F32) for size in sizes),
+        in_specs=[vmem] * 5,
+        out_specs=(hbm,) * 5,
+        scratch_shapes=[pltpu.SemaphoreType.DMA((5,))],
+    )(*(pltpu.with_memory_space_constraint(x, pltpu.VMEM) for x in results))
+    return gin.reshape(layers, cells, chans, n_phi), gspec, g_in, g_outt.T, g_bias.reshape(64)
 
 
 def solution(mesh):

time: 66.4 us -> 47.7 us (0.72)
  local copies, waits for them, and re-layouts: 15.2 us -> 0 us
  Pallas kernels: 50.1 us -> 46.9 us
    unnamed x24 -> x0, local copies, waits for them, and re-layouts: 15.2 us -> none
    pallas_call x1, Pallas kernels: 50.1 us -> 45.5 us  [local(): pl.pallas_call(functools.partial(kernel, n_dep, n_eta, chunk, factor, nor...]
    pallas_call x0 -> x1, Pallas kernels: none -> 1.4 us  [local(): pl.pallas_call(write_out, out_shape=tuple((jax.ShapeDtypeStruct(size, F32...]
where the time goes in v2:
time: 47.7 us; the launch traced here: 47.6 us
  Pallas kernels  46.9 us (98%)
  between operations  0.64 us (1%)
    pallas_call x1, Pallas kernels, local(): pl.pallas_call(functools.partial(kernel, n_dep, n_eta, chunk, factor, nor...  45.5 us
    pallas_call x1, Pallas kernels, local(): pl.pallas_call(write_out, out_shape=tuple((jax.ShapeDtypeStruct(size, F32...  1.4 us

profile of v2, /device:TPU:1, one launch (start us, length us, event | category | flops | bytes accessed | tf_op | source)
XLA Modules:
  0.0 47.6 jit_solution(1387042373743929967)
XLA Ops:
  0.6 45.5 %shard_map.137 = (f32[256,2048]{1,0:T(8,128)S(1)}, f32[2,2,8,1024]{3,2,1,0:T(8,128)S(1)}, f32[32,64]{1,0:T(8,128)S(1)}, f32[32,64]{1,0:T(8,128)S(1)}, f32[1,64]{1,0:T(1,128)S(1)}) custom-call(bf16[256,2048]{1,0:T(8,128)(2,1)} %bitcast.8, bf16[256,2048]{1,0:T(8,128)(2,1)} %bitcast.9, bf16[256,1024]{1,0:T(8,128)(2,1)} %bitcast.10, bf16[32,64]{1,0:T(8,128)(2,1)} %mlp_in_hbm.1, ...), custom_call_target="tpu_custom_call" | custom-call | tf_op jit(solution)/shard_map/pallas_call | solution.py:568
  46.2 1.4 %shard_map.138 = (f32[256,2048]{1,0:T(8,128)}, f32[2,2,8,1024]{3,2,1,0:T(8,128)}, f32[32,64]{1,0:T(8,128)}, f32[32,64]{1,0:T(8,128)}, f32[1,64]{1,0:T(1,128)}) custom-call(f32[256,2048]{1,0:T(8,128)S(1)} %get-tuple-element.15.refs_0_, f32[2,2,8,1024]{3,2,1,0:T(8,128)S(1)} %get-tuple-element.16.refs_1_, f32[32,64]{1,0:T(8,128)S(1)} %get-tuple-element.17.refs_2_, ...), custom_call_target="tpu_custom_call" | custom-call | tf_op jit(solution)/shard_map/pallas_call | solution.py:578

commit v3 on v2

--- a/solution.py
+++ b/solution.py
@@ -13,6 +13,8 @@
 F32 = jnp.float32
 BF16 = jnp.bfloat16
 MESH = pl.DeviceIdType.MESH
+CHUNK = 2048
+OUT_CHUNK = 512
 
 
 def bf(table):
@@ -79,8 +81,15 @@
     return cdf, density
 
 
-def eta_order(x):
-    blocks = [x[b * 32 : (b + 1) * 32] for b in range(8)]
+ONES = 16
+
+
+def field_rows(d):
+    return slice(d * (128 + ONES), d * (128 + ONES) + 128)
+
+
+def eta_order(x, gap=0):
+    blocks = [x[b * 32 + b // 4 * gap : (b + 1) * 32 + b // 4 * gap] for b in range(8)]
     return jnp.concatenate([blocks[d * 4 + hi * 2 + lo] for hi in range(2) for lo in range(2) for d in range(2)], axis=0)
 
 
@@ -106,6 +115,8 @@
     efwd_hbm,
     einv_hbm,
     part,
+    w_all,
+    tinv,
     gspec,
     out_in,
     out_out,
@@ -114,13 +125,11 @@
     cotan,
     weight,
     tfwd,
-    tinv,
     efwd,
     einv,
     hid,
     slope,
     gpre,
-    w_all,
     m_up,
     m_down,
     m_outt,
@@ -142,8 +151,10 @@
     arecv,
     bsend,
     brecv,
-    csend,
-    crecv,
+    absend,
+    abrecv,
+    bbsend,
+    bbrecv,
     load_sem,
     send_sem,
     recv_sem,
@@ -166,7 +177,8 @@
         pltpu.make_async_copy(src, dst, load_sem.at[n])
         for n, (src, dst) in enumerate(
             (
-                (field_hbm, field),
+                (field_hbm.at[pl.ds(0, 128)], field.at[pl.ds(0, 128)]),
+                (field_hbm.at[pl.ds(128, 128)], field.at[pl.ds(128 + ONES, 128)]),
                 (fwd_hbm, tfwd),
                 (efwd_hbm, efwd),
                 (einv_hbm, einv),
@@ -181,6 +193,7 @@
     ]
     for copy in loads:
         copy.start()
+    field[128 : 128 + ONES, :] = jnp.ones((ONES, n_phi), BF16)
 
     def eta_start(n, send, recv):
         for peer in eta_peers:
@@ -220,8 +233,8 @@
         some = pl.ds(0, count - 1)
         pltpu.make_async_copy(recv.at[some], recv.at[some], sem).wait()
 
-    def phi_forward(x, send):
-        spectra = nt(tfwd[...], eta_order(x))
+    def phi_forward(x, send, gap=0):
+        spectra = nt(tfwd[...], eta_order(x, gap))
         for q in range(4):
             for hi in range(2):
                 send[pl.ds(q * 2 + hi, n_eta, stride=8), :] = spectra[
@@ -248,13 +261,13 @@
             halves.append(jnp.concatenate(rows, axis=0).T)
         w_all[...] = cell_order(jnp.concatenate(halves, axis=0)).astype(BF16)
 
-    loads[0].wait()
-    loads[1].wait()
-    phi_forward(field[...], sends.at[0])
+    for copy in loads[:3]:
+        copy.wait()
+    phi_forward(field[...], sends.at[0], ONES)
     pl.semaphore_wait(barrier, n_eta + n_dep - 2)
     eta_start(0, sends.at[0], recvs.at[0])
 
-    for copy in loads[7:]:
+    for copy in loads[8:]:
         copy.wait()
 
     def tile_rows(x):
@@ -275,26 +288,26 @@
     bias_col[...] = jnp.broadcast_to(tile_rows(column), (256, 128))
 
     def mlp_forward(g):
-        def body(i, c):
-            cols = pl.ds(pl.multiple_of(i * chunk, chunk), chunk)
-            pre = nn(m_up[...], field[g * 128 : (g + 1) * 128, cols])
+        def body(i):
+            cols = pl.ds(i * chunk, chunk)
+            pre = nn(m_up[...], field[field_rows(g), cols])
             pre = pre + jnp.concatenate([bias_col[...]] * (chunk // 128), axis=1)
             cdf, density = cdf_and_density(pre)
             hidden = (pre * cdf).astype(BF16)
             hid[g * 256 : (g + 1) * 256, cols] = hidden
             slope[g * 256 : (g + 1) * 256, cols] = (cdf + pre * density).astype(BF16)
             part[g * 128 : (g + 1) * 128, cols] = nn(m_outt[...], hidden)
-            return c
-
-        lax.fori_loop(0, n_chunks, body, 0)
-
-    loads[4].wait()
+
+        for i in range(n_chunks):
+            body(i)
+
+    loads[5].wait()
     for ri in range(2):
         rt[ri] = weight[ri * 128 : (ri + 1) * 128, :].astype(F32).T
     mlp_forward(0)
 
-    loads[2].wait()
     loads[3].wait()
+    loads[4].wait()
     eta_wait(0, recvs.at[0])
     zx = eta_forward(recvs.at[0])
     for ri in range(2):
@@ -324,43 +337,44 @@
         for o in range(32):
             rt2[ri, o * 32 : (o + 1) * 32, :] = rt[ri, pl.ds(o, 32, stride=32), :]
 
-    loads[5].wait()
     loads[6].wait()
+    loads[7].wait()
     eta_wait(1, recvs.at[1])
     phi_inverse_lhs(recvs.at[1])
 
-    def pre_body(i, c):
-        cols = pl.ds(pl.multiple_of(i * chunk, chunk), chunk)
+    def pre_chunk(i):
+        cols = pl.ds(i * chunk, chunk)
         pre = nn(w_all[...], tinv[:, cols]) + part[:, cols]
         cdf, density = cdf_and_density(pre)
-        gpre[:, cols] = (cotan[:, cols].astype(F32) * (cdf + pre * density)).astype(BF16)
-        return c
-
-    lax.fori_loop(0, n_chunks, pre_body, 0)
+        grad = (cotan[:, cols].astype(F32) * (cdf + pre * density)).astype(BF16)
+        gpre[:, cols] = grad
+
+    for i in range(n_chunks):
+        pre_chunk(i)
     phi_forward(gpre[...], sends.at[2])
     eta_start(2, sends.at[2], recvs.at[2])
 
     def mlp_backward(g):
-        def body(i, c):
-            cols = pl.ds(pl.multiple_of(i * chunk, chunk), chunk)
+        def body(i):
+            cols = pl.ds(i * chunk, chunk)
             grad = nn(m_out[...], gpre[g * 128 : (g + 1) * 128, cols])
             slope[g * 256 : (g + 1) * 256, cols] = (
                 grad * slope[g * 256 : (g + 1) * 256, cols].astype(F32)
             ).astype(BF16)
-            return c
-
-        lax.fori_loop(0, n_chunks, body, 0)
+
+        for i in range(n_chunks):
+            body(i)
 
     def mlp_to_input(g):
-        def body(i, c):
-            cols = pl.ds(pl.multiple_of(i * chunk, chunk), chunk)
+        def body(i):
+            cols = pl.ds(i * chunk, chunk)
             rows = slice(g * 128, (g + 1) * 128)
             part[rows, cols] = cotan[rows, cols].astype(F32) + nn(
                 m_down[...], slope[g * 256 : (g + 1) * 256, cols]
             )
-            return c
-
-        lax.fori_loop(0, n_chunks, body, 0)
+
+        for i in range(n_chunks):
+            body(i)
 
     def fold(x):
         rows = x.shape[0] // 4 if x.shape[0] > 8 else 0
@@ -374,30 +388,19 @@
     sum_in = jnp.zeros((32, 128), F32)
     sum_out = jnp.zeros((32, 128), F32)
     sum_bias = jnp.zeros((8, 128), F32)
-    ones = jnp.ones((8, n_phi), BF16)
+    for g in range(2):
+        sum_out = sum_out + fold(nt(gpre[g * 128 : (g + 1) * 128, :], hid[g * 256 : (g + 1) * 256, :]))
     for g in range(2):
         mlp_backward(g)
-        grads = slope[g * 256 : (g + 1) * 256, :]
-        sum_in = sum_in + fold(nt(field[g * 128 : (g + 1) * 128, :], grads))
-        sum_out = sum_out + fold(nt(gpre[g * 128 : (g + 1) * 128, :], hid[g * 256 : (g + 1) * 256, :]))
-        sum_bias = sum_bias + fold(nt(ones, grads))
+    for g in range(2):
+        by_in = nt(field[g * 128 : g * 128 + 128 + ONES, :], slope[g * 256 : (g + 1) * 256, :])
+        sum_in = sum_in + fold(by_in[g * ONES : g * ONES + 128])
+        sum_bias = sum_bias + fold(by_in[(1 - g) * 128 : (1 - g) * 128 + 8])
     lane32 = lax.broadcasted_iota(jnp.int32, (32, 128), 1)
-    total = jnp.concatenate(
-        [jnp.where(lane32 < 64, sum_in, pltpu.roll(sum_out, 64, 1)), sum_bias, jnp.zeros((24, 128), F32)],
-        axis=0,
-    )
-    asend[...] = total.reshape(asend.shape)
-
-    for peer in dep_peers:
-        pltpu.make_async_remote_copy(
-            src_ref=asend.at[peer],
-            dst_ref=arecv.at[dep],
-            send_sem=send_sem.at[4],
-            recv_sem=recv_sem.at[4],
-            device_id=(peer, eta),
-            device_id_type=MESH,
-        ).start()
-    arecv[dep] = asend[dep]
+    asend[...] = jnp.where(lane32 < 64, sum_in, pltpu.roll(sum_out, 64, 1)).astype(BF16)
+    absend[...] = sum_bias
+    gather_start(4, "depth", asend, arecv)
+    gather_start(7, "depth", absend, abrecv)
 
     eta_wait(2, recvs.at[2])
     zg = eta_forward(recvs.at[2])
@@ -423,12 +426,16 @@
 
     mlp_to_input(0)
     blocks_wait(recv_sem.at[4], arecv, n_dep)
-    mine = arecv[0]
+    blocks_wait(recv_sem.at[7], abrecv, n_dep)
+    mine = arecv[0].astype(F32)
+    bias = abrecv[0]
     for i in range(1, n_dep):
-        mine = mine + arecv[i]
-    bsend[...] = mine
+        mine = mine + arecv[i].astype(F32)
+        bias = bias + abrecv[i]
+    bsend[...] = mine.astype(BF16)
+    bbsend[...] = bias
     gather_start(6, "eta", bsend, brecv)
-
+    gather_start(8, "eta", bbsend, bbrecv)
     mlp_to_input(1)
 
     blocks_wait(recv_sem.at[5], drecv, n_dep)
@@ -462,38 +469,38 @@
     eta_wait(3, recvs.at[3])
     phi_inverse_lhs(recvs.at[3])
 
-    def gin_body(i, c):
-        cols = pl.ds(pl.multiple_of(i * chunk, chunk), chunk)
-        part[:, cols] = part[:, cols] + nn(w_all[...], tinv[:, cols])
-        return c
-
-    lax.fori_loop(0, n_chunks, gin_body, 0)
-
     blocks_wait(recv_sem.at[6], brecv, n_eta)
-    mine = brecv[0]
+    blocks_wait(recv_sem.at[8], bbrecv, n_eta)
+    sums = brecv[0].astype(F32)
+    bias = bbrecv[0]
     for i in range(1, n_eta):
-        mine = mine + brecv[i]
-    csend[...] = mine * norm
-    gather_start(7, "depth", csend, crecv)
-    blocks_wait(recv_sem.at[7], crecv, n_dep)
-    sums = crecv[...].reshape(64, 128)
-    out_in[...] = sums[0:32, 0:64]
-    out_out[...] = pltpu.roll(sums[0:32, :], 64, 1)[:, 0:64]
-    out_bias[...] = sums[32:33, 0:64]
+        sums = sums + brecv[i].astype(F32)
+        bias = bias + bbrecv[i]
+    sums = sums * norm
+    out_in[...] = sums[:, 0:64]
+    out_out[...] = pltpu.roll(sums, 64, 1)[:, 0:64]
+    out_bias[...] = (bias * norm)[0:1, 0:64]
 
     for n in range(4):
         eta_sent(n, sends.at[n])
     blocks_wait(send_sem.at[4], arecv, n_dep)
     blocks_wait(send_sem.at[5], drecv, n_dep)
     blocks_wait(send_sem.at[6], brecv, n_eta)
-    blocks_wait(send_sem.at[7], crecv, n_dep)
-
-
-def write_out(*refs):
-    ins, outs, sem = refs[:5], refs[5:10], refs[10]
+    blocks_wait(send_sem.at[7], abrecv, n_dep)
+    blocks_wait(send_sem.at[8], bbrecv, n_eta)
+
+
+def finish(chunk, part, w_all, tinv, *refs):
+    ins, (gin, *outs), total, sem = refs[:4], refs[4:9], refs[9], refs[10]
     copies = [pltpu.make_async_copy(src, dst, sem.at[n]) for n, (src, dst) in enumerate(zip(ins, outs))]
     for copy in copies:
         copy.start()
+    for i in range(part.shape[1] // chunk):
+        cols = pl.ds(i * chunk, chunk)
+        total[:, cols] = part[:, cols] + nn(w_all[...], tinv[:, cols])
+        copy = pltpu.make_async_copy(total.at[:, cols], gin.at[:, cols], sem.at[4 + i])
+        copy.start()
+        copies.append(copy)
     for copy in copies:
         copy.wait()
 
@@ -507,24 +514,21 @@
     efwd, einv = eta_tables(n_cells, n_modes, n_eta)
     rows = layers * cells * chans
     mb = n_modes // n_dep
-    chunk = min(256, n_phi)
+    chunk, out_chunk = min(CHUNK, n_phi), min(OUT_CHUNK, n_phi)
     factor = math.sqrt(n_phi * n_cells / (owned * n_eta * n_modes))
     norm = 1.0 / math.sqrt(layers * n_dep * n_cells * n_phi)
     vmem = pl.BlockSpec(memory_space=pltpu.VMEM)
     hbm = pl.BlockSpec(memory_space=pltpu.HBM)
-    part = 64 // n_dep
     scratch = [
-        pltpu.VMEM((rows, n_phi), BF16),
+        pltpu.VMEM((rows + ONES, n_phi), BF16),
         pltpu.VMEM((rows, n_phi), BF16),
         pltpu.VMEM((4 * n_modes, 1024), BF16),
         pltpu.VMEM(fwd.shape, BF16),
-        pltpu.VMEM(inv.shape, BF16),
         pltpu.VMEM(efwd.shape, BF16),
         pltpu.VMEM(einv.shape, BF16),
         pltpu.VMEM((2 * rows, n_phi), BF16),
         pltpu.VMEM((2 * rows, n_phi), BF16),
         pltpu.VMEM((rows, n_phi), BF16),
-        pltpu.VMEM((rows, 4 * n_eta), BF16),
         pltpu.VMEM((256, 128), BF16),
         pltpu.VMEM((128, 256), BF16),
         pltpu.VMEM((128, 256), BF16),
@@ -542,17 +546,21 @@
         pltpu.VMEM((n_dep, 4, mb, 128), F32),
         pltpu.VMEM((2, 256, 1024), F32),
         pltpu.VMEM((2, 256, 128), F32),
-        pltpu.VMEM((n_dep, part, 128), F32),
-        pltpu.VMEM((n_dep, part, 128), F32),
-        pltpu.VMEM((part, 128), F32),
-        pltpu.VMEM((n_eta, part, 128), F32),
-        pltpu.VMEM((part, 128), F32),
-        pltpu.VMEM((n_dep, part, 128), F32),
-        pltpu.SemaphoreType.DMA((10,)),
-        pltpu.SemaphoreType.DMA((8,)),
-        pltpu.SemaphoreType.DMA((8,)),
+        pltpu.VMEM((32, 128), BF16),
+        pltpu.VMEM((n_dep, 32, 128), BF16),
+        pltpu.VMEM((32, 128), BF16),
+        pltpu.VMEM((n_eta, 32, 128), BF16),
+        pltpu.VMEM((8, 128), F32),
+        pltpu.VMEM((n_dep, 8, 128), F32),
+        pltpu.VMEM((8, 128), F32),
+        pltpu.VMEM((n_eta, 8, 128), F32),
+        pltpu.SemaphoreType.DMA((11,)),
+        pltpu.SemaphoreType.DMA((9,)),
+        pltpu.SemaphoreType.DMA((9,)),
     ]
     sizes = ((rows, n_phi), (2, 2, mb, 1024), (32, 64), (32, 64), (1, 64))
+    passed = [pltpu.VMEM((rows, n_phi), F32), pltpu.VMEM((rows, 4 * n_eta), BF16), pltpu.VMEM(inv.shape, BF16)]
+    passed += [pltpu.VMEM(size, F32) for size in sizes[1:]]
     operands = (
         field_in.reshape(rows, n_phi),
         grad_out.reshape(rows, n_phi),
@@ -567,20 +575,23 @@
     )
     results = pl.pallas_call(
         functools.partial(kernel, n_dep, n_eta, chunk, factor, norm),
-        out_shape=tuple(pltpu.VMEM(size, F32) for size in sizes),
+        out_shape=tuple(passed),
         in_specs=[hbm] * 10,
-        out_specs=(vmem,) * 5,
+        out_specs=(vmem,) * 7,
         scratch_shapes=scratch,
         compiler_params=pltpu.CompilerParams(
             collective_id=0, has_side_effects=True, vmem_limit_bytes=48 * 1024 * 1024
         ),
     )(*(pltpu.with_memory_space_constraint(x, pltpu.HBM) for x in operands))
     gin, gspec, g_in, g_outt, g_bias = pl.pallas_call(
-        write_out,
+        functools.partial(finish, out_chunk),
         out_shape=tuple(jax.ShapeDtypeStruct(size, F32) for size in sizes),
-        in_specs=[vmem] * 5,
+        in_specs=[vmem] * 7,
         out_specs=(hbm,) * 5,
-        scratch_shapes=[pltpu.SemaphoreType.DMA((5,))],
+        scratch_shapes=[
+            pltpu.VMEM((rows, n_phi), F32),
+            pltpu.SemaphoreType.DMA((4 + n_phi // out_chunk,)),
+        ],
     )(*(pltpu.with_memory_space_constraint(x, pltpu.VMEM) for x in results))
     return gin.reshape(layers, cells, chans, n_phi), gspec, g_in, g_outt.T, g_bias.reshape(64)
 

time: 47.7 us -> 41.3 us (0.87)
  Pallas kernels: 46.9 us -> 40.5 us
    pallas_call x1, Pallas kernels: 45.5 us -> 38.9 us  [local(): pl.pallas_call(functools.partial(kernel, n_dep, n_eta, chunk, factor, nor...]
where the time goes in v3:
time: 41.3 us; the launch traced here: 41.2 us
  Pallas kernels  40.5 us (98%)
  between operations  0.64 us (2%)
    pallas_call x1, Pallas kernels, local(): pl.pallas_call(functools.partial(kernel, n_dep, n_eta, chunk, factor, nor...  38.9 us
    pallas_call x1, Pallas kernels, local(): pl.pallas_call(functools.partial(finish, out_chunk), out_shape=tuple((jax...  1.6 us

profile of v3, /device:TPU:1, one launch (start us, length us, event | category | flops | bytes accessed | tf_op | source)
XLA Modules:
  0.0 41.2 jit_solution(15628896641238506189)
XLA Ops:
  0.6 38.9 %shard_map.137 = (f32[256,2048]{1,0:T(8,128)S(1)}, bf16[256,128]{1,0:T(8,128)(2,1)S(1)}, bf16[128,2048]{1,0:T(8,128)(2,1)S(1)}, f32[2,2,8,1024]{3,2,1,0:T(8,128)...) custom-call(bf16[256,2048]{1,0:T(8,128)(2,1)} %bitcast.8, bf16[256,2048]{1,0:T(8,128)(2,1)} %bitcast.9, ...), custom_call_target="tpu_custom_call" | custom-call | tf_op jit(solution)/shard_map/pallas_call | solution.py:576
  39.6 1.6 %shard_map.138 = (f32[256,2048]{1,0:T(8,128)}, f32[2,2,8,1024]{3,2,1,0:T(8,128)}, f32[32,64]{1,0:T(8,128)}, f32[32,64]{1,0:T(8,128)}, f32[1,64]{1,0:T(1,128)}) custom-call(f32[256,2048]{1,0:T(8,128)S(1)} %get-tuple-element.17.part, bf16[256,128]{1,0:T(8,128)(2,1)S(1)} %get-tuple-element.18.w_all, bf16[128,2048]{1,0:T(8,128)(2,1)S(1)} %get-tuple-element.19.tinv, ...), custom_call_target="tpu_custom_call" | custom-call | tf_op jit(solution)/shard_map/pallas_call | solution.py:586

commit v4 on v3

--- a/solution.py
+++ b/solution.py
@@ -14,7 +14,6 @@
 BF16 = jnp.bfloat16
 MESH = pl.DeviceIdType.MESH
 CHUNK = 2048
-OUT_CHUNK = 512
 
 
 def bf(table):
@@ -115,8 +114,6 @@
     efwd_hbm,
     einv_hbm,
     part,
-    w_all,
-    tinv,
     gspec,
     out_in,
     out_out,
@@ -125,11 +122,13 @@
     cotan,
     weight,
     tfwd,
+    tinv,
     efwd,
     einv,
     hid,
     slope,
     gpre,
+    w_all,
     m_up,
     m_down,
     m_outt,
@@ -143,8 +142,10 @@
     mlp_outt,
     sends,
     recvs,
-    dsend,
-    drecv,
+    xsend,
+    xrecv,
+    gsend,
+    grecv,
     xexp,
     gexp,
     asend,
@@ -163,6 +164,7 @@
     eta = lax.axis_index("eta")
     n_phi = field.shape[1]
     n_chunks = n_phi // chunk
+    mb = xrecv.shape[2]
 
     barrier = pltpu.get_barrier_semaphore()
 
@@ -233,6 +235,21 @@
         some = pl.ds(0, count - 1)
         pltpu.make_async_copy(recv.at[some], recv.at[some], sem).wait()
 
+    def modes_start(n, z, send, recv):
+        for ri in range(2):
+            part_z = z[:, ri * 128 : (ri + 1) * 128]
+            send[ri] = jnp.concatenate([part_z, pltpu.roll(part_z, 64, 1)], axis=0).T[0:64]
+        for peer in dep_peers:
+            pltpu.make_async_remote_copy(
+                src_ref=send.at[:, pl.ds(pl.multiple_of(peer * mb, mb), mb), :],
+                dst_ref=recv.at[dep],
+                send_sem=send_sem.at[n],
+                recv_sem=recv_sem.at[n],
+                device_id=(peer, eta),
+                device_id_type=MESH,
+            ).start()
+        recv[dep] = send[:, pl.ds(pl.multiple_of(dep * mb, mb), mb), :]
+
     def phi_forward(x, send, gap=0):
         spectra = nt(tfwd[...], eta_order(x, gap))
         for q in range(4):
@@ -312,9 +329,8 @@
     zx = eta_forward(recvs.at[0])
     for ri in range(2):
         zbuf[ri] = zx[:, ri * 128 : (ri + 1) * 128]
-    dsend_x = zx
-
-    def mix(table, sign):
+
+    def mix(table, conjugate):
         real = [jnp.zeros((32, 128), F32) for _ in range(2)]
         imag = [jnp.zeros((32, 128), F32) for _ in range(2)]
         for c in range(32):
@@ -323,15 +339,19 @@
             for d in range(2):
                 zr = zbuf[0, d * 32 + c : d * 32 + c + 1, :]
                 zi = zbuf[1, d * 32 + c : d * 32 + c + 1, :]
-                real[d] = real[d] + (zr * wr - sign * (zi * wi))
-                imag[d] = imag[d] + (zi * wr + sign * (zr * wi))
+                if conjugate:
+                    real[d] = real[d] + zr * wr + zi * wi
+                    imag[d] = imag[d] + zi * wr - zr * wi
+                else:
+                    real[d] = real[d] + zr * wr - zi * wi
+                    imag[d] = imag[d] + zi * wr + zr * wi
         return jnp.concatenate(real, axis=0), jnp.concatenate(imag, axis=0)
 
-    vr, vi = mix(rt, 1.0)
+    vr, vi = mix(rt, False)
     eta_inverse(vr, vi, sends.at[1])
     eta_start(1, sends.at[1], recvs.at[1])
 
-    dsend[:, :, 0:64] = dsend_x.T.reshape(4, 64, 64)
+    modes_start(9, zx, xsend, xrecv)
     mlp_forward(1)
     for ri in range(2):
         for o in range(32):
@@ -398,33 +418,27 @@
         sum_bias = sum_bias + fold(by_in[(1 - g) * 128 : (1 - g) * 128 + 8])
     lane32 = lax.broadcasted_iota(jnp.int32, (32, 128), 1)
     asend[...] = jnp.where(lane32 < 64, sum_in, pltpu.roll(sum_out, 64, 1)).astype(BF16)
-    absend[...] = sum_bias
+    absend[...] = sum_bias[0:1]
     gather_start(4, "depth", asend, arecv)
     gather_start(7, "depth", absend, abrecv)
+
+    blocks_wait(recv_sem.at[9], xrecv, n_dep)
+    got = xrecv[...].reshape(128, 128)
+    lane = lax.broadcasted_iota(jnp.int32, (128, 128), 1)
+    row_c = lax.rem(lax.broadcasted_iota(jnp.int32, (128, 1024), 0), 32)
+    repeat = (row_c == lax.broadcasted_iota(jnp.int32, (128, 1024), 1) // 32).astype(F32).astype(BF16)
+    for b in range(4):
+        xexp[b] = nn(jnp.where(lane // 32 == b, got, 0.0).astype(BF16), repeat)
 
     eta_wait(2, recvs.at[2])
     zg = eta_forward(recvs.at[2])
     for ri in range(2):
         zbuf[ri] = zg[:, ri * 128 : (ri + 1) * 128]
-    br, bi = mix(rt2, -1.0)
+    br, bi = mix(rt2, True)
     eta_inverse(br, bi, sends.at[3])
     eta_start(3, sends.at[3], recvs.at[3])
 
-    dsend[:, :, 64:128] = zg.T.reshape(4, 64, 64)
-    mb = drecv.shape[2]
-
-    for peer in dep_peers:
-        pltpu.make_async_remote_copy(
-            src_ref=dsend.at[:, pl.ds(pl.multiple_of(peer * mb, mb), mb), :],
-            dst_ref=drecv.at[dep],
-            send_sem=send_sem.at[5],
-            recv_sem=recv_sem.at[5],
-            device_id=(peer, eta),
-            device_id_type=MESH,
-        ).start()
-    drecv[dep] = dsend[:, pl.ds(pl.multiple_of(dep * mb, mb), mb), :]
-
-    mlp_to_input(0)
+    modes_start(5, zg, gsend, grecv)
     blocks_wait(recv_sem.at[4], arecv, n_dep)
     blocks_wait(recv_sem.at[7], abrecv, n_dep)
     mine = arecv[0].astype(F32)
@@ -436,31 +450,29 @@
     bbsend[...] = bias
     gather_start(6, "eta", bsend, brecv)
     gather_start(8, "eta", bbsend, bbrecv)
-    mlp_to_input(1)
-
-    blocks_wait(recv_sem.at[5], drecv, n_dep)
-    got = drecv[...].reshape(256, 128)
-    lane = lax.broadcasted_iota(jnp.int32, (256, 128), 1)
-    row_c = lax.rem(lax.broadcasted_iota(jnp.int32, (128, 1024), 0), 32)
-    repeat = (row_c == lax.broadcasted_iota(jnp.int32, (128, 1024), 1) // 32).astype(F32).astype(BF16)
+    for g in range(2):
+        mlp_to_input(g)
+
+    blocks_wait(recv_sem.at[5], grecv, n_dep)
+    got = grecv[...].reshape(128, 128)
     row_o = lax.rem(lax.broadcasted_iota(jnp.int32, (128, 128), 0), 32)
     tiled = (row_o == lax.rem(lax.broadcasted_iota(jnp.int32, (128, 128), 1), 32)).astype(F32).astype(BF16)
-    for d in range(2):
-        xexp[d] = nn(jnp.where(lane // 32 == d, got, 0.0).astype(BF16), repeat)
-        gexp[d] = nn(jnp.where(lane // 32 == 2 + d, got, 0.0).astype(BF16), tiled)
+    for b in range(4):
+        gexp[b] = nn(jnp.where(lane // 32 == b, got, 0.0).astype(BF16), tiled)
     for kk in range(2):
         for t in range(8):
             lanes = slice(t * 128, (t + 1) * 128)
             real = jnp.zeros((mb, 128), F32)
             imag = jnp.zeros((mb, 128), F32)
             for i in range(n_dep):
-                r0 = (i * 4 + kk) * mb
-                r1 = (i * 4 + 2 + kk) * mb
+                r0 = i * 2 * mb
+                r1 = r0 + mb
                 for d in range(2):
-                    xr = xexp[d, r0 : r0 + mb, lanes]
-                    xi = xexp[d, r1 : r1 + mb, lanes]
-                    gr = gexp[d, r0 : r0 + mb, :]
-                    gi = gexp[d, r1 : r1 + mb, :]
+                    b = kk * 2 + d
+                    xr = xexp[b, r0 : r0 + mb, lanes]
+                    xi = xexp[b, r1 : r1 + mb, lanes]
+                    gr = gexp[b, r0 : r0 + mb, :]
+                    gi = gexp[b, r1 : r1 + mb, :]
                     real = real + (xr * gr + xi * gi)
                     imag = imag + (xr * gi - xi * gr)
             gspec[0, kk, :, lanes] = real * factor
@@ -468,6 +480,7 @@
 
     eta_wait(3, recvs.at[3])
     phi_inverse_lhs(recvs.at[3])
+    part[...] = part[...] + nn(w_all[...], tinv[...])
 
     blocks_wait(recv_sem.at[6], brecv, n_eta)
     blocks_wait(recv_sem.at[8], bbrecv, n_eta)
@@ -479,28 +492,23 @@
     sums = sums * norm
     out_in[...] = sums[:, 0:64]
     out_out[...] = pltpu.roll(sums, 64, 1)[:, 0:64]
-    out_bias[...] = (bias * norm)[0:1, 0:64]
+    out_bias[...] = (bias * norm)[:, 0:64]
 
     for n in range(4):
         eta_sent(n, sends.at[n])
     blocks_wait(send_sem.at[4], arecv, n_dep)
-    blocks_wait(send_sem.at[5], drecv, n_dep)
+    blocks_wait(send_sem.at[5], grecv, n_dep)
+    blocks_wait(send_sem.at[9], xrecv, n_dep)
     blocks_wait(send_sem.at[6], brecv, n_eta)
     blocks_wait(send_sem.at[7], abrecv, n_dep)
     blocks_wait(send_sem.at[8], bbrecv, n_eta)
 
 
-def finish(chunk, part, w_all, tinv, *refs):
-    ins, (gin, *outs), total, sem = refs[:4], refs[4:9], refs[9], refs[10]
+def write_out(*refs):
+    ins, outs, sem = refs[:5], refs[5:10], refs[10]
     copies = [pltpu.make_async_copy(src, dst, sem.at[n]) for n, (src, dst) in enumerate(zip(ins, outs))]
     for copy in copies:
         copy.start()
-    for i in range(part.shape[1] // chunk):
-        cols = pl.ds(i * chunk, chunk)
-        total[:, cols] = part[:, cols] + nn(w_all[...], tinv[:, cols])
-        copy = pltpu.make_async_copy(total.at[:, cols], gin.at[:, cols], sem.at[4 + i])
-        copy.start()
-        copies.append(copy)
     for copy in copies:
         copy.wait()
 
@@ -514,7 +522,7 @@
     efwd, einv = eta_tables(n_cells, n_modes, n_eta)
     rows = layers * cells * chans
     mb = n_modes // n_dep
-    chunk, out_chunk = min(CHUNK, n_phi), min(OUT_CHUNK, n_phi)
+    chunk = min(CHUNK, n_phi)
     factor = math.sqrt(n_phi * n_cells / (owned * n_eta * n_modes))
     norm = 1.0 / math.sqrt(layers * n_dep * n_cells * n_phi)
     vmem = pl.BlockSpec(memory_space=pltpu.VMEM)
@@ -524,11 +532,13 @@
         pltpu.VMEM((rows, n_phi), BF16),
         pltpu.VMEM((4 * n_modes, 1024), BF16),
         pltpu.VMEM(fwd.shape, BF16),
+        pltpu.VMEM(inv.shape, BF16),
         pltpu.VMEM(efwd.shape, BF16),
         pltpu.VMEM(einv.shape, BF16),
         pltpu.VMEM((2 * rows, n_phi), BF16),
         pltpu.VMEM((2 * rows, n_phi), BF16),
         pltpu.VMEM((rows, n_phi), BF16),
+        pltpu.VMEM((rows, 4 * n_eta), BF16),
         pltpu.VMEM((256, 128), BF16),
         pltpu.VMEM((128, 256), BF16),
         pltpu.VMEM((128, 256), BF16),
@@ -542,25 +552,25 @@
         pltpu.VMEM((32, 64), BF16),
         pltpu.VMEM((4, 8 * n_eta, 128), F32),
         pltpu.VMEM((4, 8 * n_eta, 128), F32),
-        pltpu.VMEM((4, 64, 128), F32),
-        pltpu.VMEM((n_dep, 4, mb, 128), F32),
-        pltpu.VMEM((2, 256, 1024), F32),
-        pltpu.VMEM((2, 256, 128), F32),
+        pltpu.VMEM((2, 64, 128), F32),
+        pltpu.VMEM((n_dep, 2, mb, 128), F32),
+        pltpu.VMEM((2, 64, 128), F32),
+        pltpu.VMEM((n_dep, 2, mb, 128), F32),
+        pltpu.VMEM((4, 128, 1024), F32),
+        pltpu.VMEM((4, 128, 128), F32),
         pltpu.VMEM((32, 128), BF16),
         pltpu.VMEM((n_dep, 32, 128), BF16),
         pltpu.VMEM((32, 128), BF16),
         pltpu.VMEM((n_eta, 32, 128), BF16),
-        pltpu.VMEM((8, 128), F32),
-        pltpu.VMEM((n_dep, 8, 128), F32),
-        pltpu.VMEM((8, 128), F32),
-        pltpu.VMEM((n_eta, 8, 128), F32),
+        pltpu.VMEM((1, 128), F32),
+        pltpu.VMEM((n_dep, 1, 128), F32),
+        pltpu.VMEM((1, 128), F32),
+        pltpu.VMEM((n_eta, 1, 128), F32),
         pltpu.SemaphoreType.DMA((11,)),
-        pltpu.SemaphoreType.DMA((9,)),
-        pltpu.SemaphoreType.DMA((9,)),
+        pltpu.SemaphoreType.DMA((10,)),
+        pltpu.SemaphoreType.DMA((10,)),
     ]
     sizes = ((rows, n_phi), (2, 2, mb, 1024), (32, 64), (32, 64), (1, 64))
-    passed = [pltpu.VMEM((rows, n_phi), F32), pltpu.VMEM((rows, 4 * n_eta), BF16), pltpu.VMEM(inv.shape, BF16)]
-    passed += [pltpu.VMEM(size, F32) for size in sizes[1:]]
     operands = (
         field_in.reshape(rows, n_phi),
         grad_out.reshape(rows, n_phi),
@@ -575,23 +585,20 @@
     )
     results = pl.pallas_call(
         functools.partial(kernel, n_dep, n_eta, chunk, factor, norm),
-        out_shape=tuple(passed),
+        out_shape=tuple(pltpu.VMEM(size, F32) for size in sizes),
         in_specs=[hbm] * 10,
-        out_specs=(vmem,) * 7,
+        out_specs=(vmem,) * 5,
         scratch_shapes=scratch,
         compiler_params=pltpu.CompilerParams(
             collective_id=0, has_side_effects=True, vmem_limit_bytes=48 * 1024 * 1024
         ),
     )(*(pltpu.with_memory_space_constraint(x, pltpu.HBM) for x in operands))
     gin, gspec, g_in, g_outt, g_bias = pl.pallas_call(
-        functools.partial(finish, out_chunk),
+        write_out,
         out_shape=tuple(jax.ShapeDtypeStruct(size, F32) for size in sizes),
-        in_specs=[vmem] * 7,
+        in_specs=[vmem] * 5,
         out_specs=(hbm,) * 5,
-        scratch_shapes=[
-            pltpu.VMEM((rows, n_phi), F32),
-            pltpu.SemaphoreType.DMA((4 + n_phi // out_chunk,)),
-        ],
+        scratch_shapes=[pltpu.SemaphoreType.DMA((5,))],
     )(*(pltpu.with_memory_space_constraint(x, pltpu.VMEM) for x in results))
     return gin.reshape(layers, cells, chans, n_phi), gspec, g_in, g_outt.T, g_bias.reshape(64)
 

time: 41.3 us -> 40 us (0.969)
  Pallas kernels: 40.5 us -> 39.2 us
    pallas_call x1, Pallas kernels: 38.9 us -> 37.8 us  [local(): pl.pallas_call(functools.partial(kernel, n_dep, n_eta, chunk, factor, nor...]
where the time goes in v4:
time: 40 us; the launch traced here: 39.9 us
  Pallas kernels  39.2 us (98%)
  between operations  0.64 us (2%)
    pallas_call x1, Pallas kernels, local(): pl.pallas_call(functools.partial(kernel, n_dep, n_eta, chunk, factor, nor...  37.8 us
    pallas_call x1, Pallas kernels, local(): pl.pallas_call(write_out, out_shape=tuple((jax.ShapeDtypeStruct(size, F32...  1.4 us

profile of v4, /device:TPU:1, one launch (start us, length us, event | category | flops | bytes accessed | tf_op | source)
XLA Modules:
  0.0 39.9 jit_solution(14818105885899638656)
XLA Ops:
  0.6 37.8 %shard_map.137 = (f32[256,2048]{1,0:T(8,128)S(1)}, f32[2,2,8,1024]{3,2,1,0:T(8,128)S(1)}, f32[32,64]{1,0:T(8,128)S(1)}, f32[32,64]{1,0:T(8,128)S(1)}, f32[1,64]{1,0:T(1,128)S(1)}) custom-call(bf16[256,2048]{1,0:T(8,128)(2,1)} %bitcast.8, bf16[256,2048]{1,0:T(8,128)(2,1)} %bitcast.9, bf16[256,1024]{1,0:T(8,128)(2,1)} %bitcast.10, bf16[32,64]{1,0:T(8,128)(2,1)} %mlp_in_hbm.1, ...), custom_call_target="tpu_custom_call" | custom-call | tf_op jit(solution)/shard_map/pallas_call | solution.py:586
  38.5 1.4 %shard_map.138 = (f32[256,2048]{1,0:T(8,128)}, f32[2,2,8,1024]{3,2,1,0:T(8,128)}, f32[32,64]{1,0:T(8,128)}, f32[32,64]{1,0:T(8,128)}, f32[1,64]{1,0:T(1,128)}) custom-call(f32[256,2048]{1,0:T(8,128)S(1)} %get-tuple-element.15.refs_0_, f32[2,2,8,1024]{3,2,1,0:T(8,128)S(1)} %get-tuple-element.16.refs_1_, f32[32,64]{1,0:T(8,128)S(1)} %get-tuple-element.17.refs_2_, ...), custom_call_target="tpu_custom_call" | custom-call | tf_op jit(solution)/shard_map/pallas_call | solution.py:596

commit v5 on v4

--- a/solution.py
+++ b/solution.py
@@ -52,18 +52,14 @@
     return bf(fwd), bf(inv)
 
 
-def far_first(n_eta):
-    if n_eta != 32:
-        return [(s,) for s in range(1, n_eta)]
-    steps = [(x, z, y) for x in range(4) for z in range(2) for y in range(4)]
-    return sorted(steps[1:], key=lambda s: -(min(s[0], 4 - s[0]) + s[1] + min(s[2], 4 - s[2])))
-
-
-def eta_peer(eta, n_eta, step):
-    if len(step) == 1:
-        return lax.rem(eta + step[0], n_eta)
+def far_first(n_x, n_z):
+    steps = [(x, z, y) for x in range(n_x) for z in range(n_z) for y in range(4)]
+    return sorted(steps[1:], key=lambda s: -(min(s[0], n_x - s[0]) + s[1] + min(s[2], 4 - s[2])))
+
+
+def eta_peer(eta, n_x, step):
     x, z, y = eta // 8, lax.rem(eta // 4, 2), lax.rem(eta, 4)
-    return lax.rem(x + step[0], 4) * 8 + lax.rem(z + step[1], 2) * 4 + lax.rem(y + step[2], 4)
+    return lax.rem(x + step[0], n_x) * 8 + lax.rem(z + step[1], 2) * 4 + lax.rem(y + step[2], 4)
 
 
 def nn(a, b):
@@ -168,13 +164,18 @@
 
     barrier = pltpu.get_barrier_semaphore()
 
-    eta_peers = [eta_peer(eta, n_eta, step) for step in far_first(n_eta)]
-    dep_peers = [lax.rem(dep + s, n_dep) for s in range(1, n_dep)]
+    n_x = n_eta // 8
+    eta_peers = [eta_peer(eta, n_x, step) for step in far_first(n_x, 2)]
+    dep_peers = [lax.rem(dep + s, n_dep) for s in sorted(range(1, n_dep), key=lambda s: abs(s - n_dep // 2))]
+    other = eta_peer(eta, n_x, (0, 1, 0))
+    line = [(peer, e) for peer in dep_peers for e in (other, eta)] + [(dep, other)]
+    line_place = dep * 2 + lax.rem(eta // 4, 2)
+    plane = [(dep, eta_peer(eta, n_x, step)) for step in far_first(n_x, 1)]
+    plane_place = eta // 8 * 4 + lax.rem(eta, 4)
     for peer in eta_peers:
         pl.semaphore_signal(barrier, inc=1, device_id=(dep, peer), device_id_type=MESH)
-    for peer in dep_peers:
-        pl.semaphore_signal(barrier, inc=1, device_id=(peer, eta), device_id_type=MESH)
-
+    for peer in line[:-1]:
+        pl.semaphore_signal(barrier, inc=1, device_id=peer, device_id_type=MESH)
     loads = [
         pltpu.make_async_copy(src, dst, load_sem.at[n])
         for n, (src, dst) in enumerate(
@@ -218,18 +219,17 @@
         rows = pl.ds(0, 8 * (n_eta - 1))
         pltpu.make_async_copy(send.at[rows], send.at[rows], send_sem.at[n]).wait()
 
-    def gather_start(n, axis, block, recv):
-        me, peers = (dep, dep_peers) if axis == "depth" else (eta, eta_peers)
+    def gather_start(n, place, peers, block, recv):
         for peer in peers:
             pltpu.make_async_remote_copy(
                 src_ref=block,
-                dst_ref=recv.at[me],
+                dst_ref=recv.at[place],
                 send_sem=send_sem.at[n],
                 recv_sem=recv_sem.at[n],
-                device_id=(peer, eta) if axis == "depth" else (dep, peer),
+                device_id=peer,
                 device_id_type=MESH,
             ).start()
-        recv[me] = block[...]
+        recv[place] = block[...]
 
     def blocks_wait(sem, recv, count):
         some = pl.ds(0, count - 1)
@@ -281,7 +281,7 @@
     for copy in loads[:3]:
         copy.wait()
     phi_forward(field[...], sends.at[0], ONES)
-    pl.semaphore_wait(barrier, n_eta + n_dep - 2)
+    pl.semaphore_wait(barrier, n_eta - 1 + 2 * (n_dep - 1))
     eta_start(0, sends.at[0], recvs.at[0])
 
     for copy in loads[8:]:
@@ -340,11 +340,11 @@
                 zr = zbuf[0, d * 32 + c : d * 32 + c + 1, :]
                 zi = zbuf[1, d * 32 + c : d * 32 + c + 1, :]
                 if conjugate:
-                    real[d] = real[d] + zr * wr + zi * wi
-                    imag[d] = imag[d] + zi * wr - zr * wi
+                    real[d] = real[d] + (zr * wr + zi * wi)
+                    imag[d] = imag[d] + (zi * wr - zr * wi)
                 else:
-                    real[d] = real[d] + zr * wr - zi * wi
-                    imag[d] = imag[d] + zi * wr + zr * wi
+                    real[d] = real[d] + (zr * wr - zi * wi)
+                    imag[d] = imag[d] + (zi * wr + zr * wi)
         return jnp.concatenate(real, axis=0), jnp.concatenate(imag, axis=0)
 
     vr, vi = mix(rt, False)
@@ -419,8 +419,8 @@
     lane32 = lax.broadcasted_iota(jnp.int32, (32, 128), 1)
     asend[...] = jnp.where(lane32 < 64, sum_in, pltpu.roll(sum_out, 64, 1)).astype(BF16)
     absend[...] = sum_bias[0:1]
-    gather_start(4, "depth", asend, arecv)
-    gather_start(7, "depth", absend, abrecv)
+    gather_start(4, line_place, line, asend, arecv)
+    gather_start(7, line_place, line, absend, abrecv)
 
     blocks_wait(recv_sem.at[9], xrecv, n_dep)
     got = xrecv[...].reshape(128, 128)
@@ -439,17 +439,17 @@
     eta_start(3, sends.at[3], recvs.at[3])
 
     modes_start(5, zg, gsend, grecv)
-    blocks_wait(recv_sem.at[4], arecv, n_dep)
-    blocks_wait(recv_sem.at[7], abrecv, n_dep)
+    blocks_wait(recv_sem.at[4], arecv, 2 * n_dep)
+    blocks_wait(recv_sem.at[7], abrecv, 2 * n_dep)
     mine = arecv[0].astype(F32)
     bias = abrecv[0]
-    for i in range(1, n_dep):
+    for i in range(1, 2 * n_dep):
         mine = mine + arecv[i].astype(F32)
         bias = bias + abrecv[i]
     bsend[...] = mine.astype(BF16)
     bbsend[...] = bias
-    gather_start(6, "eta", bsend, brecv)
-    gather_start(8, "eta", bbsend, bbrecv)
+    gather_start(6, plane_place, plane, bsend, brecv)
+    gather_start(8, plane_place, plane, bbsend, bbrecv)
     for g in range(2):
         mlp_to_input(g)
 
@@ -482,11 +482,11 @@
     phi_inverse_lhs(recvs.at[3])
     part[...] = part[...] + nn(w_all[...], tinv[...])
 
-    blocks_wait(recv_sem.at[6], brecv, n_eta)
-    blocks_wait(recv_sem.at[8], bbrecv, n_eta)
+    blocks_wait(recv_sem.at[6], brecv, n_eta // 2)
+    blocks_wait(recv_sem.at[8], bbrecv, n_eta // 2)
     sums = brecv[0].astype(F32)
     bias = bbrecv[0]
-    for i in range(1, n_eta):
+    for i in range(1, n_eta // 2):
         sums = sums + brecv[i].astype(F32)
         bias = bias + bbrecv[i]
     sums = sums * norm
@@ -496,12 +496,12 @@
 
     for n in range(4):
         eta_sent(n, sends.at[n])
-    blocks_wait(send_sem.at[4], arecv, n_dep)
+    blocks_wait(send_sem.at[4], arecv, 2 * n_dep)
     blocks_wait(send_sem.at[5], grecv, n_dep)
     blocks_wait(send_sem.at[9], xrecv, n_dep)
-    blocks_wait(send_sem.at[6], brecv, n_eta)
-    blocks_wait(send_sem.at[7], abrecv, n_dep)
-    blocks_wait(send_sem.at[8], bbrecv, n_eta)
+    blocks_wait(send_sem.at[6], brecv, n_eta // 2)
+    blocks_wait(send_sem.at[7], abrecv, 2 * n_dep)
+    blocks_wait(send_sem.at[8], bbrecv, n_eta // 2)
 
 
 def write_out(*refs):
@@ -559,13 +559,13 @@
         pltpu.VMEM((4, 128, 1024), F32),
         pltpu.VMEM((4, 128, 128), F32),
         pltpu.VMEM((32, 128), BF16),
-        pltpu.VMEM((n_dep, 32, 128), BF16),
+        pltpu.VMEM((2 * n_dep, 32, 128), BF16),
         pltpu.VMEM((32, 128), BF16),
-        pltpu.VMEM((n_eta, 32, 128), BF16),
+        pltpu.VMEM((n_eta // 2, 32, 128), BF16),
         pltpu.VMEM((1, 128), F32),
-        pltpu.VMEM((n_dep, 1, 128), F32),
+        pltpu.VMEM((2 * n_dep, 1, 128), F32),
         pltpu.VMEM((1, 128), F32),
-        pltpu.VMEM((n_eta, 1, 128), F32),
+        pltpu.VMEM((n_eta // 2, 1, 128), F32),
         pltpu.SemaphoreType.DMA((11,)),
         pltpu.SemaphoreType.DMA((10,)),
         pltpu.SemaphoreType.DMA((10,)),

time: 40 us -> 39.1 us (0.978)
  Pallas kernels: 39.2 us -> 38.4 us
    pallas_call x1, Pallas kernels: 37.8 us -> 37 us  [local(): pl.pallas_call(functools.partial(kernel, n_dep, n_eta, chunk, factor, nor...]
where the time goes in v5:
time: 39.1 us; the launch traced here: 39 us
  Pallas kernels  38.4 us (98%)
  between operations  0.64 us (2%)
    pallas_call x1, Pallas kernels, local(): pl.pallas_call(functools.partial(kernel, n_dep, n_eta, chunk, factor, nor...  37 us
    pallas_call x1, Pallas kernels, local(): pl.pallas_call(write_out, out_shape=tuple((jax.ShapeDtypeStruct(size, F32...  1.4 us

profile of v5, /device:TPU:1, one launch (start us, length us, event | category | flops | bytes accessed | tf_op | source)
XLA Modules:
  0.0 39.0 jit_solution(12321557618462625356)
XLA Ops:
  0.6 37.0 %shard_map.137 = (f32[256,2048]{1,0:T(8,128)S(1)}, f32[2,2,8,1024]{3,2,1,0:T(8,128)S(1)}, f32[32,64]{1,0:T(8,128)S(1)}, f32[32,64]{1,0:T(8,128)S(1)}, f32[1,64]{1,0:T(1,128)S(1)}) custom-call(bf16[256,2048]{1,0:T(8,128)(2,1)} %bitcast.8, bf16[256,2048]{1,0:T(8,128)(2,1)} %bitcast.9, bf16[256,1024]{1,0:T(8,128)(2,1)} %bitcast.10, bf16[32,64]{1,0:T(8,128)(2,1)} %mlp_in_hbm.1, ...), custom_call_target="tpu_custom_call" | custom-call | tf_op jit(solution)/shard_map/pallas_call | solution.py:586
  37.6 1.4 %shard_map.138 = (f32[256,2048]{1,0:T(8,128)}, f32[2,2,8,1024]{3,2,1,0:T(8,128)}, f32[32,64]{1,0:T(8,128)}, f32[32,64]{1,0:T(8,128)}, f32[1,64]{1,0:T(1,128)}) custom-call(f32[256,2048]{1,0:T(8,128)S(1)} %get-tuple-element.15.refs_0_, f32[2,2,8,1024]{3,2,1,0:T(8,128)S(1)} %get-tuple-element.16.refs_1_, f32[32,64]{1,0:T(8,128)S(1)} %get-tuple-element.17.refs_2_, ...), custom_call_target="tpu_custom_call" | custom-call | tf_op jit(solution)/shard_map/pallas_call | solution.py:596

commit v6 on v5

--- a/solution.py
+++ b/solution.py
@@ -110,6 +110,8 @@
     efwd_hbm,
     einv_hbm,
     part,
+    w_all,
+    tinv,
     gspec,
     out_in,
     out_out,
@@ -118,13 +120,11 @@
     cotan,
     weight,
     tfwd,
-    tinv,
     efwd,
     einv,
     hid,
     slope,
     gpre,
-    w_all,
     m_up,
     m_down,
     m_outt,
@@ -172,10 +172,6 @@
     line_place = dep * 2 + lax.rem(eta // 4, 2)
     plane = [(dep, eta_peer(eta, n_x, step)) for step in far_first(n_x, 1)]
     plane_place = eta // 8 * 4 + lax.rem(eta, 4)
-    for peer in eta_peers:
-        pl.semaphore_signal(barrier, inc=1, device_id=(dep, peer), device_id_type=MESH)
-    for peer in line[:-1]:
-        pl.semaphore_signal(barrier, inc=1, device_id=peer, device_id_type=MESH)
     loads = [
         pltpu.make_async_copy(src, dst, load_sem.at[n])
         for n, (src, dst) in enumerate(
@@ -194,7 +190,13 @@
             )
         )
     ]
-    for copy in loads:
+    for copy in loads[:3]:
+        copy.start()
+    for peer in eta_peers:
+        pl.semaphore_signal(barrier, inc=1, device_id=(dep, peer), device_id_type=MESH)
+    for peer in line[:-1]:
+        pl.semaphore_signal(barrier, inc=1, device_id=peer, device_id_type=MESH)
+    for copy in loads[3:]:
         copy.start()
     field[128 : 128 + ONES, :] = jnp.ones((ONES, n_phi), BF16)
 
@@ -480,7 +482,6 @@
 
     eta_wait(3, recvs.at[3])
     phi_inverse_lhs(recvs.at[3])
-    part[...] = part[...] + nn(w_all[...], tinv[...])
 
     blocks_wait(recv_sem.at[6], brecv, n_eta // 2)
     blocks_wait(recv_sem.at[8], bbrecv, n_eta // 2)
@@ -504,11 +505,18 @@
     blocks_wait(send_sem.at[8], bbrecv, n_eta // 2)
 
 
-def write_out(*refs):
-    ins, outs, sem = refs[:5], refs[5:10], refs[10]
+def finish(part, w_all, tinv, *refs):
+    ins, (gin, *outs), total, sem = refs[:4], refs[4:9], refs[9], refs[10]
     copies = [pltpu.make_async_copy(src, dst, sem.at[n]) for n, (src, dst) in enumerate(zip(ins, outs))]
     for copy in copies:
         copy.start()
+    width = part.shape[1] // 4
+    for i in range(4):
+        cols = pl.ds(i * width, width)
+        total[:, cols] = part[:, cols] + nn(w_all[...], tinv[:, cols])
+        copy = pltpu.make_async_copy(total.at[:, cols], gin.at[:, cols], sem.at[4 + i])
+        copy.start()
+        copies.append(copy)
     for copy in copies:
         copy.wait()
 
@@ -532,13 +540,11 @@
         pltpu.VMEM((rows, n_phi), BF16),
         pltpu.VMEM((4 * n_modes, 1024), BF16),
         pltpu.VMEM(fwd.shape, BF16),
-        pltpu.VMEM(inv.shape, BF16),
         pltpu.VMEM(efwd.shape, BF16),
         pltpu.VMEM(einv.shape, BF16),
         pltpu.VMEM((2 * rows, n_phi), BF16),
         pltpu.VMEM((2 * rows, n_phi), BF16),
         pltpu.VMEM((rows, n_phi), BF16),
-        pltpu.VMEM((rows, 4 * n_eta), BF16),
         pltpu.VMEM((256, 128), BF16),
         pltpu.VMEM((128, 256), BF16),
         pltpu.VMEM((128, 256), BF16),
@@ -571,6 +577,7 @@
         pltpu.SemaphoreType.DMA((10,)),
     ]
     sizes = ((rows, n_phi), (2, 2, mb, 1024), (32, 64), (32, 64), (1, 64))
+    passed = [(sizes[0], F32), ((rows, 4 * n_eta), BF16), (inv.shape, BF16)] + [(size, F32) for size in sizes[1:]]
     operands = (
         field_in.reshape(rows, n_phi),
         grad_out.reshape(rows, n_phi),
@@ -585,20 +592,20 @@
     )
     results = pl.pallas_call(
         functools.partial(kernel, n_dep, n_eta, chunk, factor, norm),
-        out_shape=tuple(pltpu.VMEM(size, F32) for size in sizes),
+        out_shape=tuple(pltpu.VMEM(*spec) for spec in passed),
         in_specs=[hbm] * 10,
-        out_specs=(vmem,) * 5,
+        out_specs=(vmem,) * 7,
         scratch_shapes=scratch,
         compiler_params=pltpu.CompilerParams(
             collective_id=0, has_side_effects=True, vmem_limit_bytes=48 * 1024 * 1024
         ),
     )(*(pltpu.with_memory_space_constraint(x, pltpu.HBM) for x in operands))
     gin, gspec, g_in, g_outt, g_bias = pl.pallas_call(
-        write_out,
+        finish,
         out_shape=tuple(jax.ShapeDtypeStruct(size, F32) for size in sizes),
-        in_specs=[vmem] * 5,
+        in_specs=[vmem] * 7,
         out_specs=(hbm,) * 5,
-        scratch_shapes=[pltpu.SemaphoreType.DMA((5,))],
+        scratch_shapes=[pltpu.VMEM((rows, n_phi), F32), pltpu.SemaphoreType.DMA((8,))],
     )(*(pltpu.with_memory_space_constraint(x, pltpu.VMEM) for x in results))
     return gin.reshape(layers, cells, chans, n_phi), gspec, g_in, g_outt.T, g_bias.reshape(64)
 

time: 39.1 us -> 38.9 us (level)
  no operation moved by 1% of the time
where the time goes in v6:
time: 38.9 us; the launch traced here: 38.8 us
  Pallas kernels  38.2 us (98%)
  between operations  0.64 us (2%)
    pallas_call x1, Pallas kernels, local(): pl.pallas_call(functools.partial(kernel, n_dep, n_eta, chunk, factor, nor...  36.6 us
    pallas_call x1, Pallas kernels, local(): pl.pallas_call(finish, out_shape=tuple((jax.ShapeDtypeStruct(size, F32) f...  1.6 us

profile of v6, /device:TPU:1, one launch (start us, length us, event | category | flops | bytes accessed | tf_op | source)
XLA Modules:
  0.0 38.8 jit_solution(4180927384816338994)
XLA Ops:
  0.6 36.6 %shard_map.137 = (f32[256,2048]{1,0:T(8,128)S(1)}, bf16[256,128]{1,0:T(8,128)(2,1)S(1)}, bf16[128,2048]{1,0:T(8,128)(2,1)S(1)}, f32[2,2,8,1024]{3,2,1,0:T(8,128)...) custom-call(bf16[256,2048]{1,0:T(8,128)(2,1)} %bitcast.8, bf16[256,2048]{1,0:T(8,128)(2,1)} %bitcast.9, ...), custom_call_target="tpu_custom_call" | custom-call | tf_op jit(solution)/shard_map/pallas_call | solution.py:593
  37.2 1.6 %shard_map.138 = (f32[256,2048]{1,0:T(8,128)}, f32[2,2,8,1024]{3,2,1,0:T(8,128)}, f32[32,64]{1,0:T(8,128)}, f32[32,64]{1,0:T(8,128)}, f32[1,64]{1,0:T(1,128)}) custom-call(f32[256,2048]{1,0:T(8,128)S(1)} %get-tuple-element.17.part, bf16[256,128]{1,0:T(8,128)(2,1)S(1)} %get-tuple-element.18.w_all, bf16[128,2048]{1,0:T(8,128)(2,1)S(1)} %get-tuple-element.19.tinv, ...), custom_call_target="tpu_custom_call" | custom-call | tf_op jit(solution)/shard_map/pallas_call | solution.py:603
